TPU v7x, 256 devices: a whole 4x4x8 slice. The times are simulated.
256 devices in a mesh: gx: 4 (over y_lo, core), gy: 4 (over x), gz: 16 (over z, y_hi).
Axes of the slice: x: 4, y: 4 (y_hi: 2, y_lo: 2; y = y_hi * 2 + y_lo), z: 8, core: 2. Of those that a mesh axis runs over, the one named last changes fastest.
Arguments:
- positions: bfloat16 [4, 4, 16, 3, 432], P('gx', 'gy', 'gz'), may hold values from 0 to 15, as said below
- features: bfloat16 [4, 4, 16, 128, 432], P('gx', 'gy', 'gz'), may hold values from -6 to 6
- species: int32 [4, 4, 16, 432], P('gx', 'gy', 'gz'), may hold values from 0 to 9
- species_shift: float32 [10], replicated, may hold values from -4 to 4
- send_index: int32 [4, 4, 16, 304], P('gx', 'gy', 'gz'), may hold values from 0 to 431, as said below
- pair_target: int32 [4, 4, 16, 10, 128], P('gx', 'gy', 'gz'), may hold values from 0 to 431, as said below
- pair_source: int32 [4, 4, 16, 10, 128], P('gx', 'gy', 'gz'), may hold values from 0 to 8639, as said below
- block_count: int32 [4, 4, 16], P('gx', 'gy', 'gz'), may hold values from 3 to 10, as said below
- radial_first: bfloat16 [8, 64], replicated, may hold values from -4 to 4
- radial_second: bfloat16 [64, 64], replicated, may hold values from -1 to 1
- radial_third: bfloat16 [64, 384], replicated, may hold values from -1.5 to 1.5
- invariant_mix: bfloat16 [384, 128], replicated, may hold values from -0.3125 to 0.3125
- energy_head: bfloat16 [128], replicated, may hold values from -1 to 1
Outputs:
- energies: float32 [4, 4, 16, 432], P('gx', 'gy', 'gz')
- forces: float32 [4, 4, 16, 3, 432], P('gx', 'gy', 'gz')
Inputs may be any that keep to these rules, and one draw needn't show every extreme that they name: `positions`: the atoms of a slab fill a grid of 6 x 6 x 6 cells of side 2.5, 2 atoms to a cell. `send_index`: each slab's list holds, each once, the atoms of its outer layer of cells. `pair_target`: within a slab no pair of target and source repeats. `pair_source`: the source is never the target and lies in the target's cell or in one of the 26 cells around it; a cell beyond a face of the slab is the neighbouring slab's, and its atom then stands in that slab's slot of the ghost table. `block_count`: some slab uses all 10 blocks in every draw.
All inputs are finite; a program needn't handle non-finite values.
Results may differ from a plain program's by a relative error of at most 0.0006.
Values may be sent and summed in bfloat16 or wider, within the bound.
A program may use at most 64 MiB of HBM per device.

v0:
```python
import jax
import jax.numpy as jnp
from jax import lax
from jax.sharding import PartitionSpec as P

K = 6


cutoff_square = 25.0
basis_width = 25.0
cell_side = 2.5
message_scale = 0.15
root_three = 1.7320508075688772


def padded(array, sides, width):
    for axis, dim in sides:
        size, length = (lax.axis_size(axis), array.shape[dim])
        up = [(i, (i + 1) % size) for i in range(size)]
        down = [(j, i) for i, j in up]
        last = lax.slice_in_dim(array, length - width, length, axis=dim)
        first = lax.slice_in_dim(array, 0, width, axis=dim)
        before = lax.ppermute(last, axis, up)
        after = lax.ppermute(first, axis, down)
        array = jnp.concatenate([before, array, after], axis=dim)
    return array


def passed_along(array, axis, by):
    length = lax.axis_size(axis)
    return lax.ppermute(array, axis, [(i, (i + by) % length) for i in range(length)])


def pair_terms(rvec, source_feat, layer_one, layer_two, layer_three):
    squared = jnp.sum(rvec * rvec, axis=0)
    envelope = jnp.square(jnp.maximum(1.0 - squared / cutoff_square, 0.0))
    count_basis = layer_one.shape[1]
    centers = jnp.arange(count_basis).astype(jnp.float32) * (cutoff_square / (count_basis - 1))
    basis = (
        jnp.exp(-jnp.square(squared[None, :] - centers[:, None]) / basis_width) * envelope[None, :]
    )
    hidden_one = jax.nn.silu(jnp.dot(layer_one, basis, precision=lax.Precision.HIGHEST))
    hidden_two = jax.nn.silu(jnp.dot(layer_two, hidden_one, precision=lax.Precision.HIGHEST))
    radial = jnp.dot(layer_three, hidden_two, precision=lax.Precision.HIGHEST)
    channels = source_feat.shape[0]
    weighted = radial.reshape(3, channels, -1) * source_feat[None] * message_scale
    unit = rvec * 0.5
    ux, uy, uz = (unit[0], unit[1], unit[2])
    second = jnp.stack(
        [
            root_three * ux * uy,
            root_three * uy * uz,
            0.5 * (2.0 * uz * uz - ux * ux - uy * uy),
            root_three * ux * uz,
            0.5 * root_three * (ux * ux - uy * uy),
        ],
        0,
    )
    return jnp.concatenate(
        [weighted[0][None], weighted[1][None] * unit[:, None], weighted[2][None] * second[:, None]],
        0,
    )


def atom_energy(moments, kinds, species_shift, inv_matrix, head_vector):
    invariants = jnp.concatenate(
        [moments[0], jnp.sum(moments[1:4] ** 2, axis=0), jnp.sum(moments[4:9] ** 2, axis=0)], 0
    )
    mixed = jnp.dot(inv_matrix, invariants, precision=lax.Precision.HIGHEST)
    count_kinds = species_shift.shape[0]
    onehot = (kinds[None, :] == jnp.arange(count_kinds)[:, None]).astype(jnp.float32)
    return jnp.dot(head_vector, jax.nn.silu(mixed), precision=lax.Precision.HIGHEST) + jnp.dot(
        species_shift, onehot, precision=lax.Precision.HIGHEST
    )


def shards(
    positions,
    features,
    species,
    species_shift,
    send_index,
    pair_target,
    pair_source,
    block_count,
    radial_first,
    radial_second,
    radial_third,
    invariant_mix,
    energy_head,
):
    slab_side = cell_side * K
    own_pos = positions[0, 0, 0]
    own_feat = features[0, 0, 0]
    chosen = send_index[0, 0, 0]
    atoms = own_pos.shape[1]
    border_count = chosen.shape[0]
    width = own_feat.shape[0]
    border = jnp.concatenate(
        [jnp.take(own_feat, chosen, axis=1), jnp.take(own_pos, chosen, axis=1)], 0
    )[None, None, None]
    shells = padded(border, (("gx", 0), ("gy", 1), ("gz", 2)), 1)
    shelves = shells.reshape(27, width + 3, border_count)
    slot_ids = jnp.arange(27)
    offsets = (jnp.stack([slot_ids // 9, slot_ids // 3 % 3, slot_ids % 3], 0) - 1).astype(
        jnp.float32
    ) * slab_side
    ghost_pos = shelves[:, width:, :].astype(jnp.float32) + offsets.T[:, :, None]
    ghost_pos = ghost_pos.transpose(1, 0, 2).reshape(3, 27 * border_count)
    ghost_feat = shelves[:, :width, :].transpose(1, 0, 2).reshape(width, 27 * border_count)
    own_float = own_pos.astype(jnp.float32)
    table_pos = jnp.concatenate([own_float, ghost_pos], 1)
    table_feat = jnp.concatenate([own_feat, ghost_feat], 1)
    layers = (
        radial_first.astype(jnp.float32).T,
        radial_second.astype(jnp.float32).T,
        radial_third.astype(jnp.float32).T,
    )
    targets_all = pair_target[0, 0, 0]
    sources_all = pair_source[0, 0, 0]
    count = block_count[0, 0, 0]

    def geometry(block_index):
        target = targets_all[block_index]
        source = sources_all[block_index]
        rvec = jnp.take(table_pos, source, axis=1) - jnp.take(own_float, target, axis=1)
        source_feat = jnp.take(table_feat, source, axis=1).astype(jnp.float32)
        return (target, source, rvec, source_feat)

    def gather_step(block_index, moments):
        target, source, rvec, source_feat = geometry(block_index)
        return moments.at[:, :, target].add(pair_terms(rvec, source_feat, *layers))

    moments = lax.fori_loop(0, count, gather_step, jnp.zeros((9, width, atoms), jnp.float32))
    inv_matrix = invariant_mix.astype(jnp.float32).T
    head_vector = energy_head.astype(jnp.float32)
    kinds = species[0, 0, 0]

    def local_energy(moment_values):
        return atom_energy(moment_values, kinds, species_shift, inv_matrix, head_vector)

    energies, pull = jax.vjp(local_energy, moments)
    (moment_grad,) = pull(jnp.ones_like(energies))

    def force_step(block_index, totals):
        target, source, rvec, source_feat = geometry(block_index)
        weights_here = jnp.take(moment_grad, target, axis=2)

        def objective(displace):
            return jnp.sum(pair_terms(displace, source_feat, *layers) * weights_here)

        pull_pair = jax.grad(objective)(rvec)
        totals = totals.at[:, target].add(pull_pair)
        return totals.at[:, source].add(-pull_pair)

    totals = lax.fori_loop(
        0, count, force_step, jnp.zeros((3, atoms + 27 * border_count), jnp.float32)
    )
    spare = totals[:, atoms:].reshape(3, 3, 3, 3, border_count).transpose(1, 2, 3, 0, 4)
    arrived = [passed_along(spare[slot], "gx", step) for step, slot in ((-1, 0), (1, 2))]
    plane = spare[1] + arrived[0] + arrived[1]
    arrived = [passed_along(plane[slot], "gy", step) for step, slot in ((-1, 0), (1, 2))]
    column = plane[1] + arrived[0] + arrived[1]
    arrived = [passed_along(column[slot], "gz", step) for step, slot in ((-1, 0), (1, 2))]
    gathered = column[1] + arrived[0] + arrived[1]
    own_force = totals[:, :atoms].at[:, chosen].add(gathered)
    return (energies[None, None, None], own_force[None, None, None])


def solution(mesh):
    return jax.shard_map(
        shards,
        mesh=mesh,
        in_specs=(
            P("gx", "gy", "gz", None, None),
            P("gx", "gy", "gz", None, None),
            P("gx", "gy", "gz", None),
            P(),
            P("gx", "gy", "gz", None),
            P("gx", "gy", "gz", None, None),
            P("gx", "gy", "gz", None, None),
            P("gx", "gy", "gz"),
            P(),
            P(),
            P(),
            P(),
            P(),
        ),
        out_specs=(P("gx", "gy", "gz", None), P("gx", "gy", "gz", None, None)),
        check_vma=False,
    )
```

profile of v0, /device:TPU:126, one launch (start us, length us, event | category | flops | bytes accessed | tf_op | source)
XLA Modules:
  0.0 637.3 jit_solution(12168335106202988180)
XLA Ops:
  0.6 0.9 copy.298
  3.0 1.4 gather_fusion.8
  4.4 2.0 gather_fusion.7
  7.3 0.8 convert_bitcast_fusion
  8.2 2.6 collective-permute-done.1
  10.7 2.4 collective-permute-done
  13.2 0.9 collective-permute-start.3
  14.2 2.4 collective-permute-start.2
  16.6 10.5 %collective-permute-done.3 = bf16[3,1,1,131,304]{3,4,2,1,0:T(8,128)(2,1)S(1)} collective-permute-done((bf16[3,1,1,131,304]{3,4,2,1,0:T(8,128)(2,1)S(1)}, bf16[3,1,1,131,304]{3,4,2,1,0:T(8,128)(2,1)S(1)}, u32[]{:S(2)}, u32[]{:S(2)}) %collective-permute-start.3) | collective-permute-done | bytes 238976 | tf_op jit(solution)/shard_map/ppermute | solution.py:24
  27.5 2.1 copy.299
  29.5 1.3 collective-permute-start.5
  30.9 4.3 collective-permute-start.4
  36.2 34.5 %collective-permute-done.5 = bf16[3,3,1,131,304]{4,3,2,1,0:T(8,128)(2,1)} collective-permute-done((bf16[3,3,1,131,304]{4,3,2,1,0:T(8,128)(2,1)}, bf16[3,3,1,131,304]{4,3,2,1,0:T(8,128)(2,1)}, u32[]{:S(2)}, u32[]{:S(2)}) %collective-permute-start.5) | collective-permute-done | bytes 716864 | tf_op jit(solution)/shard_map/ppermute | solution.py:24
  70.8 2.4 copy.302
  73.2 1.3 collective-permute-done.4
  74.5 2.4 copy.301
  76.9 2.8 pad_maximum_fusion
  80.1 2.2 convert_add_fusion
  82.3 3.1 copy.325
  85.6 2.8 copy.307
  88.3 1.8 pad_maximum_fusion.1
  90.1 2.0 broadcast_in_dim.105
  92.1 72.8 %while.20 = (s32[]{:T(128)}, f32[9,128,432]{1,0,2:T(8,128)}, s32[]{:T(128)}, s32[10,128]{1,0:T(8,128)S(1)}, s32[10,128]{1,0:T(8,128)S(1)}, /*index=5*/f32[3,8640...) while((s32[]{:T(128)}, f32[9,128,432]{1,0,2:T(8,128)}, ...), condition=%wide.region_3.7_spmd, body=%wide.region_0.6_spmd.sunk | while | flops 45610260 | bytes 6038391 | solution.py:134
  93.7 2.9 gather_fusion.1
  97.9 2.6 gather_fusion.2
  101.8 14.4 %scatter_fusion = f32[9,128,432]{1,0,2:T(8,128)} fusion(f32[9,128,432]{1,0,2:T(8,128)} %get-tuple-element.654, s32[128]{0:T(128)S(1)} %fusion.161, f32[128,9,128]{2,1,0:T(8,128)S(1)} %maximum_bitcast_fusion.3), kind=kCustom, calls=%fused_computation.9.clone.1 | custom fusion | flops 147456 | bytes 1769984 | tf_op jit(solution)/shard_map/while/body/scatter-add | solution.py:132
  117.7 2.9 gather_fusion.1
  121.9 2.6 gather_fusion.2
  125.8 14.4 %scatter_fusion = f32[9,128,432]{1,0,2:T(8,128)} fusion(f32[9,128,432]{1,0,2:T(8,128)} %get-tuple-element.654, s32[128]{0:T(128)S(1)} %fusion.161, f32[128,9,128]{2,1,0:T(8,128)S(1)} %maximum_bitcast_fusion.3), kind=kCustom, calls=%fused_computation.9.clone.1 | custom fusion | flops 147456 | bytes 1769984 | tf_op jit(solution)/shard_map/while/body/scatter-add | solution.py:132
  141.7 2.9 gather_fusion.1
  145.9 2.6 gather_fusion.2
  149.8 14.4 %scatter_fusion = f32[9,128,432]{1,0,2:T(8,128)} fusion(f32[9,128,432]{1,0,2:T(8,128)} %get-tuple-element.654, s32[128]{0:T(128)S(1)} %fusion.161, f32[128,9,128]{2,1,0:T(8,128)S(1)} %maximum_bitcast_fusion.3), kind=kCustom, calls=%fused_computation.9.clone.1 | custom fusion | flops 147456 | bytes 1769984 | tf_op jit(solution)/shard_map/while/body/scatter-add | solution.py:132
  164.9 2.6 copy.309
  167.7 1.6 slice.89
  170.6 2.5 copy.313
  173.1 2.2 broadcast_in_dim.112
  175.3 78.0 %while.21 = (s32[]{:T(128)}, f32[3,8640]{0,1:T(8,128)}, s32[]{:T(128)}, s32[10,128]{1,0:T(8,128)S(1)}, s32[10,128]{1,0:T(8,128)S(1)}, /*index=5*/f32[3,8640]{0,1...) while((s32[]{:T(128)}, f32[3,8640]{0,1:T(8,128)}, ...), condition=%wide.region_16.20_spmd, body=%wide.region_6.19_spmd.sunk | while | flops 90919440 | bytes 6970026 | solution.py:156
  176.7 2.9 gather_fusion.4
  180.2 2.6 gather_fusion.5
  183.8 2.6 gather_fusion.6
  190.0 5.5 scatter_fusion.1
  195.6 5.5 scatter_fusion.2
  202.5 2.9 gather_fusion.4
  206.0 2.6 gather_fusion.5
  209.5 2.6 gather_fusion.6
  215.8 5.5 scatter_fusion.1
  221.3 5.5 scatter_fusion.2
  228.3 2.9 gather_fusion.4
  231.8 2.6 gather_fusion.5
  235.3 2.6 gather_fusion.6
  241.5 5.5 scatter_fusion.1
  247.1 5.5 scatter_fusion.2
  253.3 3.7 slice.93
  256.9 4.6 copy.326
  261.6 198.3 %collective-permute-start.7 = (f32[3,3,3,304]{3,2,1,0:T(4,128)S(1)}, f32[3,3,3,304]{3,2,1,0:T(4,128)S(1)}, u32[]{:S(2)}, u32[]{:S(2)}) collective-permute-start(f32[3,3,3,304]{3,2,1,0:T(4,128)S(1)} %copy.317), channel_id=1, source_target_pairs={{0,64},{64,128},{128,192},{192,0},{1,65},{65,129},{129,193},{193,1... | collective-permute-start | bytes 98504 | tf_op jit(solution)/shard_map/ppermute | solution.py:31
  460.0 96.6 %collective-permute-start.6 = (f32[3,3,3,304]{3,2,1,0:T(4,128)S(1)}, f32[3,3,3,304]{3,2,1,0:T(4,128)S(1)}, u32[]{:S(2)}, u32[]{:S(2)}) collective-permute-start(f32[3,3,3,304]{3,2,1,0:T(4,128)S(1)} %copy.315), channel_id=1, source_target_pairs={{0,192},{64,0},{128,64},{192,128},{1,193},{65,1},{129,65},{193,129... | collective-permute-start | bytes 98504 | tf_op jit(solution)/shard_map/ppermute | solution.py:31
  556.6 1.7 collective-permute-done.7
  558.5 2.7 collective-permute-start.8
  561.4 1.5 collective-permute-done.9
  563.6 63.3 %collective-permute-start.11 = (f32[3,304]{1,0:T(4,128)S(1)}, f32[3,304]{1,0:T(4,128)S(1)}, u32[]{:S(2)}, u32[]{:S(2)}) collective-permute-start(f32[3,304]{1,0:T(4,128)S(1)} %bitcast.284), channel_id=1, source_target_pairs={{0,1},{1,2},{2,3},{3,4},{4,5},{5,6},{6,7},{7,8},{8,9},{9,10},{10,1... | collective-permute-start | bytes 10952 | tf_op jit(solution)/shard_map/ppermute | solution.py:31
  627.2 1.0 slice.92
  628.8 5.4 collective-permute-done.10
  634.3 2.3 scatter_fusion.3
  636.6 0.7 copy.324
  (310 shorter events, 34.9 us)
Async XLA Ops:
  0.6 168.6 %copy-start = (bf16[384,128]{1,0:T(8,128)(2,1)S(1)}, bf16[384,128]{1,0:T(8,128)(2,1)}, u32[]{:S(2)}) copy-start(bf16[384,128]{1,0:T(8,128)(2,1)} %param.34) | copy-start | bytes 294916
  6.6 28.7 %copy-start.6 = (bf16[64,64]{1,0:T(8,128)(2,1)S(1)}, bf16[64,64]{1,0:T(8,128)(2,1)}, u32[]{:S(2)}) copy-start(bf16[64,64]{1,0:T(8,128)(2,1)} %param.32) | copy-start | bytes 24580
  6.7 28.9 %copy-start.13 = (bf16[128]{0:T(256)(128)(2,1)S(1)}, bf16[128]{0:T(256)(128)(2,1)}, u32[]{:S(2)}) copy-start(bf16[128]{0:T(256)(128)(2,1)} %param.35) | copy-start | bytes 772
  6.7 29.5 %copy-start.10 = (bf16[8,64]{1,0:T(8,128)(2,1)S(1)}, bf16[8,64]{1,0:T(8,128)(2,1)}, u32[]{:S(2)}) copy-start(bf16[8,64]{1,0:T(8,128)(2,1)} %param.31) | copy-start | bytes 3076
  6.7 4.0 collective-permute-start.1
  7.0 6.2 collective-permute-start
  8.1 28.1 %copy-start.8 = (s32[1,1,1,10,128]{4,2,3,1,0:T(1,128)S(1)}, s32[1,1,1,10,128]{4,2,3,1,0:T(1,128)}, u32[]{:S(2)}) copy-start(s32[1,1,1,10,128]{4,2,3,1,0:T(1,128)} %param.29) | copy-start | bytes 15364
  8.1 28.1 %copy-start.9 = (s32[1,1,1,10,128]{4,2,3,1,0:T(1,128)S(1)}, s32[1,1,1,10,128]{4,2,3,1,0:T(1,128)}, u32[]{:S(2)}) copy-start(s32[1,1,1,10,128]{4,2,3,1,0:T(1,128)} %param.28) | copy-start | bytes 15364
  10.7 24.7 %copy-start.4 = (bf16[1,1,1,131,304]{3,4,2,1,0:T(8,128)(2,1)}, bf16[1,1,1,131,304]{3,4,2,1,0:T(8,128)(2,1)S(1)}, u32[]{:S(2)}) copy-start(bf16[1,1,1,131,304]{3,4,2,1,0:T(8,128)(2,1)S(1)} %collective-permute-done.1) | copy-start | bytes 238948
  13.1 23.1 %copy-start.5 = (bf16[1,1,1,131,304]{3,4,2,1,0:T(8,128)(2,1)}, bf16[1,1,1,131,304]{3,4,2,1,0:T(8,128)(2,1)S(1)}, u32[]{:S(2)}) copy-start(bf16[1,1,1,131,304]{3,4,2,1,0:T(8,128)(2,1)S(1)} %collective-permute-done) | copy-start | bytes 238948
  13.2 13.8 %collective-permute-start.3 = (bf16[3,1,1,131,304]{3,4,2,1,0:T(8,128)(2,1)S(1)}, bf16[3,1,1,131,304]{3,4,2,1,0:T(8,128)(2,1)S(1)}, u32[]{:S(2)}, u32[]{:S(2)}) collective-permute-start(bf16[3,1,1,131,304]{3,4,2,1,0:T(8,128)(2,1)S(1)} %pad_maximum_fusion.3), channel_id=1, source_target_pairs={{16,0},{32,16},{48,32},{0,48},{17,1},{33,17},{49,33},{1,49},{18,2}... | collective-permute-start | bytes 716840 | tf_op jit(solution)/shard_map/ppermute | solution.py:24
  14.2 12.9 %collective-permute-start.2 = (bf16[3,1,1,131,304]{3,4,2,1,0:T(8,128)(2,1)S(1)}, bf16[3,1,1,131,304]{3,4,2,1,0:T(8,128)(2,1)S(1)}, u32[]{:S(2)}, u32[]{:S(2)}) collective-permute-start(bf16[3,1,1,131,304]{3,4,2,1,0:T(8,128)(2,1)S(1)} %pad_maximum_fusion.3), channel_id=1, source_target_pairs={{0,16},{16,32},{32,48},{48,0},{1,17},{17,33},{33,49},{49,1},{2,18}... | collective-permute-start | bytes 716840 | tf_op jit(solution)/shard_map/ppermute | solution.py:23
  27.1 46.1 %copy-start.2 = (bf16[3,1,1,131,304]{3,4,2,1,0:T(8,128)(2,1)}, bf16[3,1,1,131,304]{3,4,2,1,0:T(8,128)(2,1)S(1)}, u32[]{:S(2)}) copy-start(bf16[3,1,1,131,304]{3,4,2,1,0:T(8,128)(2,1)S(1)} %collective-permute-done.3) | copy-start | bytes 716836
  27.1 46.1 %copy-start.3 = (bf16[3,1,1,131,304]{3,4,2,1,0:T(8,128)(2,1)}, bf16[3,1,1,131,304]{3,4,2,1,0:T(8,128)(2,1)S(1)}, u32[]{:S(2)}) copy-start(bf16[3,1,1,131,304]{3,4,2,1,0:T(8,128)(2,1)S(1)} %collective-permute-done.2) | copy-start | bytes 716836
  29.5 41.3 %collective-permute-start.5 = (bf16[3,3,1,131,304]{4,3,2,1,0:T(8,128)(2,1)}, bf16[3,3,1,131,304]{4,3,2,1,0:T(8,128)(2,1)}, u32[]{:S(2)}, u32[]{:S(2)}) collective-permute-start(bf16[3,3,1,131,304]{4,3,2,1,0:T(8,128)(2,1)} %copy.299), channel_id=1, source_target_pairs={{1,0},{2,1},{3,2},{4,3},{5,4},{6,5},{7,6},{8,7},{9,8},{10,9},{11,1... | collective-permute-start | bytes 2150504 | tf_op jit(solution)/shard_map/ppermute | solution.py:24
  30.9 43.6 %collective-permute-start.4 = (bf16[3,3,1,131,304]{4,3,2,1,0:T(8,128)(2,1)}, bf16[3,3,1,131,304]{4,3,2,1,0:T(8,128)(2,1)}, u32[]{:S(2)}, u32[]{:S(2)}) collective-permute-start(bf16[3,3,1,131,304]{4,3,2,1,0:T(8,128)(2,1)} %copy.299), channel_id=1, source_target_pairs={{0,1},{1,2},{2,3},{3,4},{4,5},{5,6},{6,7},{7,8},{8,9},{9,10},{10,1... | collective-permute-start | bytes 2150504 | tf_op jit(solution)/shard_map/ppermute | solution.py:23
  82.3 6.0 copy-start.1
  164.9 4.8 copy-start.15
  173.1 2.2 copy-start.7
  256.9 304.3 %copy-start.11 = (s32[1,1,1,432]{3,2,1,0:T(1,128)S(1)}, s32[1,1,1,432]{3,2,1,0:T(1,128)}, u32[]{:S(2)}) copy-start(s32[1,1,1,432]{3,2,1,0:T(1,128)} %param.25) | copy-start | bytes 5188
  256.9 304.3 %copy-start.12 = (f32[10]{0:T(128)S(1)}, f32[10]{0:T(128)}, u32[]{:S(2)}) copy-start(f32[10]{0:T(128)} %param.26) | copy-start | bytes 124
  256.9 370.0 %copy-start.14 = (bf16[128]{0:T(256)(128)(2,1)S(1)}, bf16[128]{0:T(256)(128)(2,1)}, u32[]{:S(2)}) copy-start(bf16[128]{0:T(256)(128)(2,1)} %param.35) | copy-start | bytes 772
  261.6 296.6 %collective-permute-start.7 = (f32[3,3,3,304]{3,2,1,0:T(4,128)S(1)}, f32[3,3,3,304]{3,2,1,0:T(4,128)S(1)}, u32[]{:S(2)}, u32[]{:S(2)}) collective-permute-start(f32[3,3,3,304]{3,2,1,0:T(4,128)S(1)} %copy.317), channel_id=1, source_target_pairs={{0,64},{64,128},{128,192},{192,0},{1,65},{65,129},{129,193},{193,1... | collective-permute-start | bytes 98504 | tf_op jit(solution)/shard_map/ppermute | solution.py:31
  460.0 98.4 %collective-permute-start.6 = (f32[3,3,3,304]{3,2,1,0:T(4,128)S(1)}, f32[3,3,3,304]{3,2,1,0:T(4,128)S(1)}, u32[]{:S(2)}, u32[]{:S(2)}) collective-permute-start(f32[3,3,3,304]{3,2,1,0:T(4,128)S(1)} %copy.315), channel_id=1, source_target_pairs={{0,192},{64,0},{128,64},{192,128},{1,193},{65,1},{129,65},{193,129... | collective-permute-start | bytes 98504 | tf_op jit(solution)/shard_map/ppermute | solution.py:31
  558.4 4.4 collective-permute-start.9
  558.5 5.0 collective-permute-start.8
  563.6 65.2 %collective-permute-start.11 = (f32[3,304]{1,0:T(4,128)S(1)}, f32[3,304]{1,0:T(4,128)S(1)}, u32[]{:S(2)}, u32[]{:S(2)}) collective-permute-start(f32[3,304]{1,0:T(4,128)S(1)} %bitcast.284), channel_id=1, source_target_pairs={{0,1},{1,2},{2,3},{3,4},{4,5},{5,6},{6,7},{7,8},{8,9},{9,10},{10,1... | collective-permute-start | bytes 10952 | tf_op jit(solution)/shard_map/ppermute | solution.py:31
  626.9 7.2 %collective-permute-start.10 = (f32[3,304]{1,0:T(4,128)S(1)}, f32[3,304]{1,0:T(4,128)S(1)}, u32[]{:S(2)}, u32[]{:S(2)}) collective-permute-start(f32[3,304]{1,0:T(4,128)S(1)} %bitcast.285), channel_id=1, source_target_pairs={{0,15},{1,0},{2,1},{3,2},{4,3},{5,4},{6,5},{7,6},{8,7},{9,8},{10,9... | collective-permute-start | bytes 10952 | tf_op jit(solution)/shard_map/ppermute | solution.py:31
where the time goes:
time: 643 us; the launch traced here: 637 us
  starting transfers between devices  371 us (58%)
  other arithmetic  97.9 us (15%)
  local copies, waits for them, and re-layouts  91.4 us (14%)
  waiting for transfers between devices  60.7 us (9%)
  matrix products  9.04 us (1%)
  loops' own time  6.64 us (1%)
    ppermute x6, starting transfers between devices, passed_along(): lax.ppermute(array, axis, [(i, (i + by) % length) for i in range(length)])  361 us
    ppermute x3, waiting for transfers between devices, padded(): after = lax.ppermute(first, axis, down)  47.6 us
    scatter-add x3, other arithmetic, gather_step(): return moments.at[:, :, target].add(pair_terms(rvec, source_feat, *layers))  43.3 us
    gather x12, local copies, waits for them, and re-layouts, geometry(): jnp.take(table_pos, source, axis=1) - jnp.take(own_float, target, axis=1)  17.9 us
    scatter-add x3, other arithmetic, force_step(): totals = totals.at[:, target].add(pull_pair)  16.4 us
    scatter-add x3, other arithmetic, force_step(): return totals.at[:, source].add(-pull_pair)  16.4 us
    gather x6, local copies, waits for them, and re-layouts, geometry(): source_feat = jnp.take(table_feat, source, axis=1).astype(jnp.float32)  15.4 us
  transfers between devices with their start and end apart: 12, of which 10 were waited for; matrix products, arithmetic and copies ran while one was open for 1% of the time, Pallas kernels for 0%

commit v1 on v0

v1 whole, which is shorter than its diff:
```python
import functools

import jax
import jax.numpy as jnp
import numpy as np
from jax import lax
from jax.experimental import pallas as pl
from jax.experimental.pallas import tpu as pltpu
from jax.sharding import PartitionSpec as P

A = 432
AP = 512
G = 304
CH = 128
NB = 10
PB = 128
BL = 256
STEPS = NB * PB // BL
RH = 64
NRB = 8
SPECIES = 10
GT = 1280
SENT = 1088
CELL = 2.5
SIDE = 15.0
CUT = 25.0
MID = 152.0
SCALE = 0.15
ROOT3 = 1.7320508075688772

F32 = jnp.float32
BF16 = jnp.bfloat16
MESH = pl.DeviceIdType.MESH
NN = (((1,), (0,)), ((), ()))
NT = (((1,), (1,)), ((), ()))


def offset_of(slot):
    return (slot // 9 - 1, slot // 3 % 3 - 1, slot % 3 - 1)


def places():
    by_kind = {1: [], 2: [], 3: []}
    for slot in range(27):
        if slot != 13:
            by_kind[sum(abs(c) for c in offset_of(slot))].append(slot)
    out = []
    for i, slot in enumerate(by_kind[1]):
        out.append((slot, 96, 96 * i, 128 * i))
    for i, slot in enumerate(by_kind[2]):
        out.append((slot, 32, 576 + 32 * i, 768 + 32 * i))
    for i, slot in enumerate(by_kind[3]):
        out.append((slot, 16, 960 + 16 * i, 1152 + 16 * i))
    return out


PLACES = places()


def dot(a, b, dims=NN):
    return lax.dot_general(a, b, dims, preferred_element_type=F32)


def iota(shape, dim):
    return lax.broadcasted_iota(jnp.int32, shape, dim)


def high_low(x):
    high = x.astype(BF16).astype(F32)
    return high, x - high


def neighbour(slot, sign):
    where = []
    for axis, size, step in zip(("gx", "gy", "gz"), (4, 4, 16), offset_of(slot)):
        me = lax.axis_index(axis)
        where.append(lax.rem(me + (size + sign * step), size) if step else me)
    return tuple(where)


def enter():
    barrier = pltpu.get_barrier_semaphore()
    for slot, *_ in PLACES:
        pl.semaphore_signal(
            barrier, inc=1, device_id=neighbour(slot, 1), device_id_type=MESH
        )
    return barrier


def choose(pos_ref, feat_ref, list_ref, pick_ref, send_ref):
    pos = pos_ref[...].astype(F32)
    entry = (iota((A, G), 0) == list_ref[...]).astype(BF16)
    ids = iota((8, G), 1).astype(F32)
    coded = jnp.where(ids < MID, ids - MID, ids - (MID - 1.0))
    code = dot(coded.astype(BF16), entry, NT)
    member = (code[0:1] != 0.0).astype(F32)
    slots = iota((32, A), 0)
    ix = (slots >= 9).astype(jnp.int32) + (slots >= 18).astype(jnp.int32)
    rest = slots - 9 * ix
    iy = (rest >= 3).astype(jnp.int32) + (rest >= 6).astype(jnp.int32)
    iz = rest - 3 * iy
    strict = member
    closed = member
    for axis, index in enumerate((ix, iy, iz)):
        x = pos[axis : axis + 1]
        one = jnp.ones((1, A), F32)
        strict = strict * jnp.where(
            index == 0,
            (x > SIDE - CELL).astype(F32),
            jnp.where(index == 2, (x < CELL).astype(F32), one),
        )
        closed = closed * jnp.where(
            index == 0,
            (x >= SIDE - CELL).astype(F32),
            jnp.where(index == 2, (x <= CELL).astype(F32), one),
        )
    both = jnp.concatenate([strict, closed - strict], 0)
    upper = (iota((A, A), 0) <= iota((A, A), 1)).astype(BF16)
    count = dot(both.astype(BF16), upper)
    total = count[:32, A - 1 : A]
    rank = jnp.where(
        strict > 0.0,
        count[:32] - 1.0,
        jnp.where(closed > 0.0, total + count[32:] - 1.0, -1.0),
    )
    for slot, rows, _, lane in PLACES:
        tall = 128 if rows == 96 else rows
        step = iota((tall, A), 0)
        step = jnp.where(step < rows - 4, step, -2).astype(F32)
        pick_ref[lane : lane + tall, :] = (step == rank[slot : slot + 1]).astype(BF16)
    meta = jnp.concatenate([jnp.zeros((4, A), F32), pos, code[0:1]], 0).astype(BF16)
    for slot, rows, row, lane in PLACES:
        if rows == 96:
            block = dot(pick_ref[lane : lane + 128, :], feat_ref[...], NT)
            told = dot(meta, pick_ref[lane : lane + 128, :], NT)
            out = jnp.concatenate([block[:88], block[88:96] + told], 0)
            send_ref[row : row + 96, :] = out.astype(BF16)
    for group in range(4):
        start = 768 + 128 * group
        rows = 32 if group < 3 else 16
        block = dot(pick_ref[start : start + 128, :], feat_ref[...], NT)
        told = dot(meta, pick_ref[start : start + 128, :], NT)
        pieces = []
        for i in range(128 // rows):
            pieces.append(block[rows * i : rows * i + rows - 8])
            pieces.append(block[rows * i + rows - 8 : rows * (i + 1)] + told)
        row = 576 + 128 * group
        send_ref[row : row + 128, :] = jnp.concatenate(pieces, 0).astype(BF16)


def exchange_kernel(
    pos_ref, feat_ref, list_ref, pick_ref, got_ref, send_ref, send_sem, recv_sem
):
    barrier = enter()
    choose(pos_ref, feat_ref, list_ref, pick_ref, send_ref)
    pl.semaphore_wait(barrier, 26)
    copies = []
    for i, (slot, rows, row, _) in enumerate(PLACES):
        copies.append(
            pltpu.make_async_remote_copy(
                src_ref=send_ref.at[row : row + rows, :],
                dst_ref=got_ref.at[row : row + rows, :],
                send_sem=send_sem.at[i],
                recv_sem=recv_sem.at[i],
                device_id=neighbour(slot, -1),
                device_id_type=MESH,
            )
        )
        copies[-1].start()
    for copy in copies:
        copy.wait()


def group_lanes(tiles, width):
    lane = iota(tiles[0].shape, 1)
    out = tiles[0]
    for i in range(1, len(tiles)):
        out = jnp.where(lane >= width * i, tiles[i], out)
    return out


def ghost_table(got_ref, table_ref, key_ref):
    tiles = [[] for _ in range(10)]
    for place in PLACES:
        tiles[place[3] // 128].append(place)
    for t, members in enumerate(tiles):
        width = 128 // len(members)
        row, rows = members[0][2], members[0][1]
        if rows == 96:
            feats = jnp.concatenate(
                [got_ref[row : row + 96, :].astype(F32), jnp.zeros((32, CH), F32)], 0
            )
        else:
            feats = got_ref[row : row + 128, :].astype(F32)
        table_ref[0:CH, 128 * t : 128 * (t + 1)] = feats.T.astype(BF16)
        told, offs = [], []
        for slot, rows, row, _ in members:
            told.append(got_ref[row + rows - 16 : row + rows, :].astype(F32)[8:16])
        told = group_lanes(told, width)
        sub = iota((8, 128), 0)
        for slot, *_ in members:
            o = offset_of(slot)
            offs.append(
                jnp.where(
                    sub == 0,
                    float(o[0]),
                    jnp.where(sub == 1, float(o[1]), jnp.where(sub == 2, float(o[2]), 0.0)),
                )
            )
        offs = group_lanes(offs, width)
        base = group_lanes(
            [jnp.full((8, 128), float(A + G * slot), F32) for slot, *_ in members], width
        )
        table_ref[CH : CH + 16, 128 * t : 128 * (t + 1)] = jnp.concatenate(
            [told, offs], 0
        ).astype(BF16)
        code = told[7:8]
        index = jnp.where(code < 0.0, code + MID, code + (MID - 1.0)) + base[0:1]
        key = jnp.where(code == 0.0, -5.0, index)
        column = jnp.broadcast_to(key, (128, 128)).T.astype(jnp.int32)
        key_ref[128 * t : 128 * (t + 1), :] = jnp.concatenate([column, column], 1)


def silu_parts(z):
    s = 0.5 * jnp.tanh(0.5 * z) + 0.5
    h = z * s
    return h, s + h * (1.0 - s)


def stack_high_low(x):
    return jnp.concatenate(high_low(x), 0).astype(BF16)


def main_kernel(
    count_ref,
    shift_ref,
    pos_ref,
    feat_ref,
    got_ref,
    species_ref,
    target_ref,
    source_ref,
    first_ref,
    second_ref,
    third_ref,
    mix_ref,
    head_ref,
    energy_ref,
    own_ref,
    ghost_ref,
    own_table,
    table,
    keys,
    from_own,
    from_ghost,
    to_own,
    radial_ref,
    slope_ref,
    geom_ref,
    terms_ref,
    moments,
    grads,
    back_ref,
):
    count = count_ref[0]
    ghost_table(got_ref, table, keys)
    own_table[...] = jnp.zeros_like(own_table)
    own_table[0:CH, 0:A] = feat_ref[...]
    pos = jnp.concatenate([pos_ref[...].astype(F32), jnp.zeros((13, A), F32)], 0)
    own_table[CH : CH + 16, 0:A] = pos.astype(BF16)
    first = first_ref[...].astype(F32).T
    first = jnp.concatenate([first, first], 1).astype(BF16)
    second = second_ref[...].astype(F32).T
    second = jnp.concatenate([second, second], 1).astype(BF16)
    third = third_ref[...].astype(F32).T
    third = jnp.concatenate([third, third], 1).astype(BF16)
    moments[...] = jnp.zeros_like(moments)

    def pair_rows(ref, b):
        return jnp.concatenate([ref[pl.ds(2 * b, 1), :], ref[pl.ds(2 * b + 1, 1), :]], 1)

    def forward(b, carry):
        source = pair_rows(source_ref, b)
        target = pair_rows(target_ref, b)
        live = 2 * b + (iota((1, BL), 1) >= PB).astype(jnp.int32) < count
        target = jnp.where(live, target, -1)
        atoms = iota((AP, BL), 0)
        pick_own = (atoms == source).astype(BF16)
        pick_ghost = (keys[...] == source).astype(BF16)
        pick_target = (atoms == target).astype(BF16)
        from_own[b] = pick_own
        from_ghost[b] = pick_ghost
        to_own[b, 0:AP, :] = pick_target
        to_own[b, AP : 2 * AP, :] = pick_target
        near = dot(own_table[...], pick_own)
        far = dot(table[...], pick_ghost)
        feats = (near[:CH] + far[:CH]) * SCALE
        here = dot(own_table[CH : CH + 16, :], pick_target)
        r = (
            (near[CH : CH + 3] + far[CH + 4 : CH + 7])
            + SIDE * far[CH + 8 : CH + 11]
            - here[0:3]
        )
        q = r[0:1] * r[0:1] + r[1:2] * r[1:2] + r[2:3] * r[2:3]
        keep = jnp.maximum(1.0 - q / CUT, 0.0)
        envelope = keep * keep
        d_envelope = keep * (-2.0 / CUT)
        centers = iota((NRB, BL), 0).astype(F32) * (CUT / (NRB - 1))
        away = q - centers
        bump = jnp.exp(-(away * away) / CUT)
        basis = bump * envelope
        d_basis = bump * (d_envelope - (2.0 / CUT) * away * envelope)
        z = dot(first, jnp.concatenate([stack_high_low(basis), stack_high_low(d_basis)], 1))
        h, slope = silu_parts(z[:, :BL])
        d = slope * z[:, BL:]
        z = dot(second, jnp.concatenate([stack_high_low(h), stack_high_low(d)], 1))
        h, slope = silu_parts(z[:, :BL])
        d = slope * z[:, BL:]
        z = dot(third, jnp.concatenate([stack_high_low(h), stack_high_low(d)], 1))
        ux, uy, uz = 0.5 * r[0:1], 0.5 * r[1:2], 0.5 * r[2:3]
        harmonics = [
            [None],
            [ux, uy, uz],
            [
                ROOT3 * ux * uy,
                ROOT3 * uy * uz,
                0.5 * (2.0 * uz * uz - ux * ux - uy * uy),
                ROOT3 * ux * uz,
                0.5 * ROOT3 * (ux * ux - uy * uy),
            ],
        ]
        geom_ref[b] = jnp.concatenate([r, jnp.zeros((5, BL), F32)], 0)
        row = 0
        for order in range(3):
            weighted = z[CH * order : CH * (order + 1), :BL] * feats
            radial_ref[b, CH * order : CH * (order + 1), :] = weighted
            slope_ref[b, CH * order : CH * (order + 1), :] = (
                z[CH * order : CH * (order + 1), BL:] * feats
            )
            for harmonic in harmonics[order]:
                term = weighted if harmonic is None else weighted * harmonic
                high, low = high_low(term)
                terms_ref[row : row + CH, 0:BL] = high.astype(BF16)
                terms_ref[row : row + CH, BL : 2 * BL] = low.astype(BF16)
                row += CH
        twice = jnp.concatenate([pick_target, pick_target], 1)
        moments[...] += dot(terms_ref[...], twice, NT)
        return carry

    lax.fori_loop(0, STEPS, forward, 0)

    def moment(i):
        return moments[CH * i : CH * (i + 1), :]

    squares = []
    for low, high in ((1, 4), (4, 9)):
        total = moment(low) * moment(low)
        for i in range(low + 1, high):
            total = total + moment(i) * moment(i)
        squares.append(total)
    invariants = jnp.concatenate([moment(0)] + squares, 0)
    mix = mix_ref[...]
    mix_t = mix.astype(F32).T.astype(BF16)
    high, low = high_low(invariants)
    mixed = dot(mix_t, high.astype(BF16)) + dot(mix_t, low.astype(BF16))
    head = jnp.broadcast_to(head_ref[...].astype(F32), (128, 128)).T
    head = jnp.concatenate([head] * 4, 1)
    h, slope = silu_parts(mixed)
    energy = jnp.sum(head * h, axis=0, keepdims=True)[:, :A]
    kinds = species_ref[...]
    for k in range(SPECIES):
        energy = energy + jnp.where(kinds == k, shift_ref[k], 0.0)
    energy_ref[...] = energy
    d_mixed = stack_high_low(head * slope)
    d_inv = dot(jnp.concatenate([mix, mix], 1), d_mixed)
    for i in range(9):
        order = 0 if i == 0 else (1 if i < 4 else 2)
        grad = d_inv[CH * order : CH * (order + 1)]
        if order:
            grad = 2.0 * moment(i) * grad
        high, low = high_low(grad)
        grads[CH * i : CH * (i + 1), 0:AP] = high.astype(BF16)
        grads[CH * i : CH * (i + 1), AP : 2 * AP] = low.astype(BF16)
    own_ref[...] = jnp.zeros_like(own_ref)
    ghost_ref[...] = jnp.zeros_like(ghost_ref)

    def backward(b, carry):
        back_ref[...] = dot(grads[...], to_own[b])
        r = geom_ref[b]
        along, across = [], []
        for i in range(9):
            order = 0 if i == 0 else (1 if i < 4 else 2)
            grad = back_ref[CH * i : CH * (i + 1), :]
            if order:
                along.append(
                    jnp.sum(
                        radial_ref[b, CH * order : CH * (order + 1), :] * grad,
                        axis=0,
                        keepdims=True,
                    )
                )
            across.append(
                jnp.sum(
                    slope_ref[b, CH * order : CH * (order + 1), :] * grad,
                    axis=0,
                    keepdims=True,
                )
            )
        ux, uy, uz = 0.5 * r[0:1], 0.5 * r[1:2], 0.5 * r[2:3]
        ax, ay, az, b0, b1, b2, b3, b4 = along
        dq = (
            across[0]
            + ux * across[1]
            + uy * across[2]
            + uz * across[3]
            + (ROOT3 * ux * uy) * across[4]
            + (ROOT3 * uy * uz) * across[5]
            + (0.5 * (2.0 * uz * uz - ux * ux - uy * uy)) * across[6]
            + (ROOT3 * ux * uz) * across[7]
            + (0.5 * ROOT3 * (ux * ux - uy * uy)) * across[8]
        )
        gx = ax + ROOT3 * (uy * b0 + uz * b3 + ux * b4) - ux * b2
        gy = ay + ROOT3 * (ux * b0 + uz * b1 - uy * b4) - uy * b2
        gz = az + ROOT3 * (uy * b1 + ux * b3) + 2.0 * uz * b2
        px = 0.5 * gx + 2.0 * dq * r[0:1]
        py = 0.5 * gy + 2.0 * dq * r[1:2]
        pz = 0.5 * gz + 2.0 * dq * r[2:3]
        pull = jnp.concatenate([px, py, pz, jnp.zeros((5, BL), F32)], 0)
        pull = stack_high_low(pull)
        own = dot(pull, to_own[b, 0:AP, :] - from_own[b], NT)
        ghost = dot(pull, from_ghost[b], NT)
        own_ref[...] += own[:8] + own[8:]
        ghost_ref[...] -= ghost[:8] + ghost[8:]
        return carry

    lax.fori_loop(0, STEPS, backward, 0)


def return_kernel(ghost_ref, own_ref, pick_ref, force_ref, got_ref, send_sem, recv_sem):
    barrier = enter()
    pl.semaphore_wait(barrier, 26)
    copies = []
    for i, (slot, rows, _, lane) in enumerate(PLACES):
        start = lane // 128 * 128
        copies.append(
            pltpu.make_async_remote_copy(
                src_ref=ghost_ref.at[:, start : start + 128],
                dst_ref=got_ref.at[i],
                send_sem=send_sem.at[i],
                recv_sem=recv_sem.at[i],
                device_id=neighbour(slot, 1),
                device_id_type=MESH,
            )
        )
        copies[-1].start()
    for copy in copies:
        copy.wait()
    tiles = [[] for _ in range(10)]
    for i, place in enumerate(PLACES):
        tiles[place[3] // 128].append(got_ref[i])
    tiles = [group_lanes(members, 128 // len(members)) for members in tiles]
    sums = dot(stack_high_low(jnp.concatenate(tiles, 1)), pick_ref[...])
    total = own_ref[:, :A] + sums[:8] + sums[8:]
    force_ref[...] = total[:3]


def vmem():
    return pl.BlockSpec(memory_space=pltpu.VMEM)


def smem():
    return pl.BlockSpec(memory_space=pltpu.SMEM)


def shape(dims, kind=F32):
    return jax.ShapeDtypeStruct(dims, kind)


def shards(
    positions,
    features,
    species,
    species_shift,
    send_index,
    pair_target,
    pair_source,
    block_count,
    radial_first,
    radial_second,
    radial_third,
    invariant_mix,
    energy_head,
):
    pos = positions.reshape(3, A)
    feat = features.reshape(CH, A)
    pick, got = pl.pallas_call(
        exchange_kernel,
        out_shape=(shape((GT, A), BF16), shape((SENT, CH), BF16)),
        in_specs=[vmem()] * 3,
        out_specs=(vmem(), vmem()),
        scratch_shapes=[
            pltpu.VMEM((SENT, CH), BF16),
            pltpu.SemaphoreType.DMA((26,)),
            pltpu.SemaphoreType.DMA((26,)),
        ],
        compiler_params=pltpu.CompilerParams(
            collective_id=0, has_side_effects=True, vmem_limit_bytes=24 * 2**20
        ),
        name="exchange",
    )(pos, feat, send_index.reshape(1, G))
    energies, own, ghost = pl.pallas_call(
        main_kernel,
        out_shape=(shape((1, A)), shape((8, AP)), shape((8, GT))),
        in_specs=[smem()] * 2 + [vmem()] * 11,
        out_specs=(vmem(), vmem(), vmem()),
        scratch_shapes=[
            pltpu.VMEM((CH + 16, AP), BF16),
            pltpu.VMEM((CH + 16, GT), BF16),
            pltpu.VMEM((GT, BL), jnp.int32),
            pltpu.VMEM((STEPS, AP, BL), BF16),
            pltpu.VMEM((STEPS, GT, BL), BF16),
            pltpu.VMEM((STEPS, 2 * AP, BL), BF16),
            pltpu.VMEM((STEPS, 3 * CH, BL), F32),
            pltpu.VMEM((STEPS, 3 * CH, BL), F32),
            pltpu.VMEM((STEPS, 8, BL), F32),
            pltpu.VMEM((9 * CH, 2 * BL), BF16),
            pltpu.VMEM((9 * CH, AP), F32),
            pltpu.VMEM((9 * CH, 2 * AP), BF16),
            pltpu.VMEM((9 * CH, BL), F32),
        ],
        compiler_params=pltpu.CompilerParams(vmem_limit_bytes=48 * 2**20),
        name="interact",
    )(
        block_count.reshape(1),
        species_shift,
        pos,
        feat,
        got,
        species.reshape(1, A),
        pair_target.reshape(NB, PB),
        pair_source.reshape(NB, PB),
        radial_first,
        radial_second,
        radial_third,
        invariant_mix,
        energy_head.reshape(1, CH),
    )
    forces = pl.pallas_call(
        return_kernel,
        out_shape=shape((3, A)),
        in_specs=[vmem()] * 3,
        out_specs=vmem(),
        scratch_shapes=[
            pltpu.VMEM((26, 8, 128), F32),
            pltpu.SemaphoreType.DMA((26,)),
            pltpu.SemaphoreType.DMA((26,)),
        ],
        compiler_params=pltpu.CompilerParams(
            collective_id=1, has_side_effects=True, vmem_limit_bytes=24 * 2**20
        ),
        name="give_back",
    )(ghost, own, pick)
    return (energies.reshape(1, 1, 1, A), forces.reshape(1, 1, 1, 3, A))


def solution(mesh):
    split = ("gx", "gy", "gz")
    return jax.shard_map(
        shards,
        mesh=mesh,
        in_specs=(
            P(*split, None, None),
            P(*split, None, None),
            P(*split, None),
            P(),
            P(*split, None),
            P(*split, None, None),
            P(*split, None, None),
            P(*split),
            P(),
            P(),
            P(),
            P(),
            P(),
        ),
        out_specs=(P(*split, None), P(*split, None, None)),
        check_vma=False,
    )
```

time: 643 us -> 57 us (0.09)
  the two profiles are of different devices: /device:TPU:126 before, /device:TPU:1 now
where the time goes in v1:
time: 57 us; the launch traced here: 56.6 us
  Pallas kernels  45.8 us (80%)
  local copies, waits for them, and re-layouts  9.43 us (17%)
  between operations  1.33 us (2%)
    pallas_call x1, Pallas kernels, shards(): pl.pallas_call(main_kernel, out_shape=(shape((1, A)), shape((8, AP)), sha...  19.3 us
    pallas_call x1, Pallas kernels, shards(): pl.pallas_call(exchange_kernel, out_shape=(shape((GT, A), BF16), shape((S...  16 us
    pallas_call x1, Pallas kernels, shards(): pl.pallas_call(return_kernel, out_shape=shape((3, A)), in_specs=[vmem()]...  10.5 us
    unnamed x23, local copies, waits for them, and re-layouts  9.43 us

profile of v1, /device:TPU:1, one launch (start us, length us, event | category | flops | bytes accessed | tf_op | source)
XLA Modules:
  0.0 56.6 jit_solution(11914379646004680103)
XLA Ops:
  1.3 0.7 %copy_bitcast_fusion = (s32[10,128]{1,0:T(8,128)S(1)}, s32[10,128]{1,0:T(8,128)S(1)}) fusion(s32[1,1,1,10,128]{4,2,3,1,0:T(1,128)} %param.19, s32[1,1,1,10,128]{4,2,3,1,0:T(1,128)} %param.18), kind=kLoop, calls=%fused_computation | loop fusion | bytes 20480
  2.0 1.0 %copy.15 = bf16[1,1,1,128,432]{4,3,2,1,0:T(8,128)(2,1)S(1)} copy(bf16[1,1,1,128,432]{3,4,2,1,0:T(8,128)(2,1)} %param.14) | data formatting | bytes 221184 | tf_op args[1]
  3.0 0.0 copy-start.2
  3.0 0.7 %copy-done.2 = bf16[1,1,1,3,432]{4,3,2,1,0:T(4,128)(2,1)S(1)} copy-done((bf16[1,1,1,3,432]{4,3,2,1,0:T(4,128)(2,1)S(1)}, bf16[1,1,1,3,432]{4,3,2,1,0:T(4,128)(2,1)}, u32[]{:S(2)}) %copy-start.2) | copy-done | bytes 2616
  3.7 0.0 copy-start.7
  3.7 0.7 %copy-done.7 = s32[1,1,1,304]{3,2,1,0:T(1,128)S(1)} copy-done((s32[1,1,1,304]{3,2,1,0:T(1,128)S(1)}, s32[1,1,1,304]{3,2,1,0:T(1,128)}, u32[]{:S(2)}) %copy-start.7) | copy-done | bytes 1240
  4.4 16.0 %exchange.1 = (bf16[1280,432]{1,0:T(8,128)(2,1)S(1)}, bf16[1088,128]{1,0:T(8,128)(2,1)S(1)}) custom-call(bf16[3,432]{1,0:T(4,128)(2,1)S(1)} %bitcast.16, bf16[128,432]{1,0:T(8,128)(2,1)S(1)} %bitcast.13, s32[1,304]{1,0:T(1,128)S(1)} %bitcast.19), custom_call_target="tpu_custom_call" | custom-call | tf_op jit(solution)/shard_map/exchange/pallas_call | solution.py:496
  20.4 0.0 copy-start
  20.4 0.9 %copy-done = bf16[384,128]{1,0:T(8,128)(2,1)S(1)} copy-done((bf16[384,128]{1,0:T(8,128)(2,1)S(1)}, bf16[384,128]{1,0:T(8,128)(2,1)}, u32[]{:S(2)}) %copy-start) | copy-done | bytes 98328
  21.3 0.0 copy-start.1
  21.3 0.8 %copy-done.1 = bf16[64,384]{1,0:T(8,128)(2,1)S(1)} copy-done((bf16[64,384]{1,0:T(8,128)(2,1)S(1)}, bf16[64,384]{1,0:T(8,128)(2,1)}, u32[]{:S(2)}) %copy-start.1) | copy-done | bytes 49176
  22.1 0.0 copy-start.3
  22.1 0.7 %copy-done.3 = bf16[1,1,1,3,432]{4,3,2,1,0:T(4,128)(2,1)S(1)} copy-done((bf16[1,1,1,3,432]{4,3,2,1,0:T(4,128)(2,1)S(1)}, bf16[1,1,1,3,432]{4,3,2,1,0:T(4,128)(2,1)}, u32[]{:S(2)}) %copy-start.3) | copy-done | bytes 2616
  22.8 0.0 copy-start.4
  22.8 0.7 %copy-done.4 = bf16[64,64]{1,0:T(8,128)(2,1)S(1)} copy-done((bf16[64,64]{1,0:T(8,128)(2,1)S(1)}, bf16[64,64]{1,0:T(8,128)(2,1)}, u32[]{:S(2)}) %copy-start.4) | copy-done | bytes 8216
  23.5 0.0 copy-start.5
  23.5 0.7 %copy-done.5 = s32[1,1,1,432]{3,2,1,0:T(1,128)S(1)} copy-done((s32[1,1,1,432]{3,2,1,0:T(1,128)S(1)}, s32[1,1,1,432]{3,2,1,0:T(1,128)}, u32[]{:S(2)}) %copy-start.5) | copy-done | bytes 1752
  24.2 0.0 copy-start.6
  24.2 0.7 %copy-done.6 = bf16[8,64]{1,0:T(8,128)(2,1)S(1)} copy-done((bf16[8,64]{1,0:T(8,128)(2,1)S(1)}, bf16[8,64]{1,0:T(8,128)(2,1)}, u32[]{:S(2)}) %copy-start.6) | copy-done | bytes 1048
  24.9 0.0 copy-start.8
  24.9 0.7 %copy-done.8 = f32[10]{0:T(128)S(1)} copy-done((f32[10]{0:T(128)S(1)}, f32[10]{0:T(128)}, u32[]{:S(2)}) %copy-start.8) | copy-done | bytes 64
  25.5 0.0 copy-start.9
  25.5 0.7 %copy-done.9 = bf16[128]{0:T(256)(128)(2,1)S(1)} copy-done((bf16[128]{0:T(256)(128)(2,1)S(1)}, bf16[128]{0:T(256)(128)(2,1)}, u32[]{:S(2)}) %copy-start.9) | copy-done | bytes 280
  26.2 19.3 %interact.1 = (f32[1,432]{1,0:T(1,128)}, f32[8,512]{1,0:T(8,128)S(1)}, f32[8,1280]{1,0:T(8,128)S(1)}) custom-call(s32[1]{0:T(128)} %bitcast.12.count_ref, f32[10]{0:T(128)S(1)} %copy-done.8, bf16[3,432]{1,0:T(4,128)(2,1)S(1)} %bitcast.17, bf16[128,432]{1,0:T(8,128)(2,1)S(1)} %bitcast.14, bf16[1088,128]{1,0:T(8,128)(2,1)S(1)} %get-tuple-element.7.got_ref, ...), custom_call_target="tpu_custom_call" | custom-call | tf_op jit(solution)/shard_map/interact/pallas_call | solution.py:511
  45.5 10.5 %give_back.1 = f32[3,432]{1,0:T(4,128)S(1)} custom-call(f32[8,1280]{1,0:T(8,128)S(1)} %get-tuple-element.9.ghost_ref, f32[8,512]{1,0:T(8,128)S(1)} %get-tuple-element.10.own_ref, bf16[1280,432]{1,0:T(8,128)(2,1)S(1)} %get-tuple-element.11.pick_ref), custom_call_target="tpu_custom_call" | custom-call | tf_op jit(solution)/shard_map/give_back/pallas_call | solution.py:548
  56.0 0.6 %copy.16 = f32[1,1,1,3,432]{4,2,3,1,0:T(1,128)} copy(f32[1,1,1,3,432]{4,3,2,1,0:T(4,128)S(1)} %bitcast.15) | data formatting | bytes 10368
Async XLA Ops:
  3.0 0.7 %copy-start.2 = (bf16[1,1,1,3,432]{4,3,2,1,0:T(4,128)(2,1)S(1)}, bf16[1,1,1,3,432]{4,3,2,1,0:T(4,128)(2,1)}, u32[]{:S(2)}) copy-start(bf16[1,1,1,3,432]{4,3,2,1,0:T(4,128)(2,1)} %param.13) | copy-start | bytes 7780
  3.7 0.7 %copy-start.7 = (s32[1,1,1,304]{3,2,1,0:T(1,128)S(1)}, s32[1,1,1,304]{3,2,1,0:T(1,128)}, u32[]{:S(2)}) copy-start(s32[1,1,1,304]{3,2,1,0:T(1,128)} %param.17) | copy-start | bytes 3652
  20.4 0.9 %copy-start = (bf16[384,128]{1,0:T(8,128)(2,1)S(1)}, bf16[384,128]{1,0:T(8,128)(2,1)}, u32[]{:S(2)}) copy-start(bf16[384,128]{1,0:T(8,128)(2,1)} %mix_ref.1) | copy-start | bytes 294916
  21.3 0.8 %copy-start.1 = (bf16[64,384]{1,0:T(8,128)(2,1)S(1)}, bf16[64,384]{1,0:T(8,128)(2,1)}, u32[]{:S(2)}) copy-start(bf16[64,384]{1,0:T(8,128)(2,1)} %third_ref.1) | copy-start | bytes 147460
  22.1 0.7 %copy-start.3 = (bf16[1,1,1,3,432]{4,3,2,1,0:T(4,128)(2,1)S(1)}, bf16[1,1,1,3,432]{4,3,2,1,0:T(4,128)(2,1)}, u32[]{:S(2)}) copy-start(bf16[1,1,1,3,432]{4,3,2,1,0:T(4,128)(2,1)} %param.13) | copy-start | bytes 7780
  22.8 0.7 %copy-start.4 = (bf16[64,64]{1,0:T(8,128)(2,1)S(1)}, bf16[64,64]{1,0:T(8,128)(2,1)}, u32[]{:S(2)}) copy-start(bf16[64,64]{1,0:T(8,128)(2,1)} %second_ref.1) | copy-start | bytes 24580
  23.5 0.7 %copy-start.5 = (s32[1,1,1,432]{3,2,1,0:T(1,128)S(1)}, s32[1,1,1,432]{3,2,1,0:T(1,128)}, u32[]{:S(2)}) copy-start(s32[1,1,1,432]{3,2,1,0:T(1,128)} %param.15) | copy-start | bytes 5188
  24.2 0.7 %copy-start.6 = (bf16[8,64]{1,0:T(8,128)(2,1)S(1)}, bf16[8,64]{1,0:T(8,128)(2,1)}, u32[]{:S(2)}) copy-start(bf16[8,64]{1,0:T(8,128)(2,1)} %first_ref.1) | copy-start | bytes 3076
  24.9 0.7 %copy-start.8 = (f32[10]{0:T(128)S(1)}, f32[10]{0:T(128)}, u32[]{:S(2)}) copy-start(f32[10]{0:T(128)} %shift_ref.1) | copy-start | bytes 124
  25.5 0.7 %copy-start.9 = (bf16[128]{0:T(256)(128)(2,1)S(1)}, bf16[128]{0:T(256)(128)(2,1)}, u32[]{:S(2)}) copy-start(bf16[128]{0:T(256)(128)(2,1)} %param.25) | copy-start | bytes 772

commit v2 on v1

v2 whole, which is shorter than its diff:
```python
import functools

import jax
import jax.numpy as jnp
import numpy as np
from jax import lax
from jax.experimental import pallas as pl
from jax.experimental.pallas import tpu as pltpu
from jax.sharding import PartitionSpec as P

A = 432
AP = 512
G = 304
CH = 128
NB = 10
PB = 128
BL = 256
STEPS = NB * PB // BL
NP = NB * PB
RH = 64
NRB = 8
SPECIES = 10
GT = 1280
SENT = 1088
CELL = 2.5
SIDE = 15.0
CUT = 25.0
MID = 152.0
SCALE = 0.15
ROOT3 = 1.7320508075688772

F32 = jnp.float32
BF16 = jnp.bfloat16
MESH = pl.DeviceIdType.MESH
KEY = jnp.int32
NN = (((1,), (0,)), ((), ()))
NT = (((1,), (1,)), ((), ()))


def offset_of(slot):
    return (slot // 9 - 1, slot // 3 % 3 - 1, slot % 3 - 1)


def places():
    by_kind = {1: [], 2: [], 3: []}
    for slot in range(27):
        if slot != 13:
            by_kind[sum(abs(c) for c in offset_of(slot))].append(slot)
    out = []
    for i, slot in enumerate(by_kind[1]):
        out.append((slot, 96, 96 * i, 128 * i))
    for i, slot in enumerate(by_kind[2]):
        out.append((slot, 32, 576 + 32 * i, 768 + 32 * i))
    for i, slot in enumerate(by_kind[3]):
        out.append((slot, 16, 960 + 16 * i, 1152 + 16 * i))
    return out


PLACES = places()


def dot(a, b, dims=NN):
    return lax.dot_general(a, b, dims, preferred_element_type=F32)


def iota(shape, dim):
    return lax.broadcasted_iota(jnp.int32, shape, dim)


def high_low(x):
    high = x.astype(BF16).astype(F32)
    return high, x - high


def neighbour(slot, sign):
    where = []
    for axis, size, step in zip(("gx", "gy", "gz"), (4, 4, 16), offset_of(slot)):
        me = lax.axis_index(axis)
        where.append(lax.rem(me + (size + sign * step), size) if step else me)
    return tuple(where)


def enter():
    barrier = pltpu.get_barrier_semaphore()
    for slot, *_ in PLACES:
        pl.semaphore_signal(
            barrier, inc=1, device_id=neighbour(slot, 1), device_id_type=MESH
        )
    return barrier


def choose(pos_ref, feat_ref, list_ref, pick_ref, send_ref):
    pos = pos_ref[...].astype(F32)
    entry = (iota((A, G), 0) == list_ref[...]).astype(BF16)
    ids = iota((8, G), 1).astype(F32)
    coded = jnp.where(ids < MID, ids - MID, ids - (MID - 1.0))
    code = dot(coded.astype(BF16), entry, NT)
    member = (code[0:1] != 0.0).astype(F32)
    slots = iota((32, A), 0)
    ix = (slots >= 9).astype(jnp.int32) + (slots >= 18).astype(jnp.int32)
    rest = slots - 9 * ix
    iy = (rest >= 3).astype(jnp.int32) + (rest >= 6).astype(jnp.int32)
    iz = rest - 3 * iy
    strict = member
    closed = member
    for axis, index in enumerate((ix, iy, iz)):
        x = pos[axis : axis + 1]
        one = jnp.ones((1, A), F32)
        strict = strict * jnp.where(
            index == 0,
            (x > SIDE - CELL).astype(F32),
            jnp.where(index == 2, (x < CELL).astype(F32), one),
        )
        closed = closed * jnp.where(
            index == 0,
            (x >= SIDE - CELL).astype(F32),
            jnp.where(index == 2, (x <= CELL).astype(F32), one),
        )
    both = jnp.concatenate([strict, closed - strict], 0)
    upper = (iota((A, A), 0) <= iota((A, A), 1)).astype(BF16)
    count = dot(both.astype(BF16), upper)
    total = count[:32, A - 1 : A]
    rank = jnp.where(
        strict > 0.0,
        count[:32] - 1.0,
        jnp.where(closed > 0.0, total + count[32:] - 1.0, -1.0),
    )
    for slot, rows, _, lane in PLACES:
        tall = 128 if rows == 96 else rows
        step = iota((tall, A), 0)
        step = jnp.where(step < rows - 4, step, -2).astype(F32)
        pick_ref[lane : lane + tall, :] = (step == rank[slot : slot + 1]).astype(BF16)
    meta = jnp.concatenate([jnp.zeros((4, A), F32), pos, code[0:1]], 0).astype(BF16)
    feat = feat_ref[...]
    for slot, rows, row, lane in PLACES:
        if rows == 96:
            block = dot(pick_ref[lane : lane + 96, :], feat)
            told = dot(meta, pick_ref[lane : lane + 128, :], NT)
            out = jnp.concatenate([block[:88], block[88:96] + told], 0)
            send_ref[row : row + 96, :] = out.astype(BF16)
    for group in range(4):
        start = 768 + 128 * group
        rows = 32 if group < 3 else 16
        block = dot(pick_ref[start : start + 128, :], feat)
        told = dot(meta, pick_ref[start : start + 128, :], NT)
        pieces = []
        for i in range(128 // rows):
            pieces.append(block[rows * i : rows * i + rows - 8])
            pieces.append(block[rows * i + rows - 8 : rows * (i + 1)] + told)
        row = 576 + 128 * group
        send_ref[row : row + 128, :] = jnp.concatenate(pieces, 0).astype(BF16)


def group_lanes(tiles, width):
    lane = iota(tiles[0].shape, 1)
    out = tiles[0]
    for i in range(1, len(tiles)):
        out = jnp.where(lane >= width * i, tiles[i], out)
    return out


def ghost_table(got_ref, table_ref, key_ref):
    tiles = [[] for _ in range(10)]
    for place in PLACES:
        tiles[place[3] // 128].append(place)
    for t, members in enumerate(tiles):
        width = 128 // len(members)
        row, rows = members[0][2], members[0][1]
        if rows == 96:
            feats = jnp.concatenate(
                [got_ref[row : row + 96, :].astype(F32), jnp.zeros((32, CH), F32)], 0
            )
        else:
            feats = got_ref[row : row + 128, :].astype(F32)
        table_ref[0:CH, 128 * t : 128 * (t + 1)] = feats.T.astype(BF16)
        told, offs = [], []
        for slot, rows, row, _ in members:
            told.append(got_ref[row + rows - 16 : row + rows, :].astype(F32)[8:16])
        told = group_lanes(told, width)
        sub = iota((8, 128), 0)
        for slot, *_ in members:
            o = offset_of(slot)
            offs.append(
                jnp.where(
                    sub == 0,
                    float(o[0]),
                    jnp.where(sub == 1, float(o[1]), jnp.where(sub == 2, float(o[2]), 0.0)),
                )
            )
        offs = group_lanes(offs, width)
        base = group_lanes(
            [jnp.full((8, 128), float(A + G * slot), F32) for slot, *_ in members], width
        )
        table_ref[CH : CH + 16, 128 * t : 128 * (t + 1)] = jnp.concatenate(
            [told, offs], 0
        ).astype(BF16)
        code = told[7:8]
        index = jnp.where(code < 0.0, code + MID, code + (MID - 1.0)) + base[0:1]
        key = jnp.where(code == 0.0, -5.0, index)
        column = jnp.broadcast_to(key, (128, 128)).T.astype(KEY)
        key_ref[128 * t : 128 * (t + 1), :] = jnp.concatenate([column, column], 1)


def silu_parts(z):
    s = 0.5 * jnp.tanh(0.5 * z) + 0.5
    h = z * s
    return h, s + h * (1.0 - s)


def stack_high_low(x):
    return jnp.concatenate(high_low(x), 0).astype(BF16)


def span(b):
    return pl.ds(pl.multiple_of(b * BL, BL), BL)


def pair_rows(ref, b):
    return jnp.concatenate([ref[2 * b], ref[2 * b + 1]], 1)


def twice_across(ref):
    x = ref[...].astype(F32).T
    return jnp.concatenate([x, x], 1).astype(BF16)


def prepare(r):
    r.own_table[...] = jnp.zeros_like(r.own_table)
    feat = r.feat[...].astype(F32).T
    r.own_table[0:CH, 0:A] = feat.astype(BF16)
    pos = jnp.concatenate([r.pos[...].astype(F32), jnp.zeros((13, A), F32)], 0)
    r.own_table[CH : CH + 16, 0:A] = pos.astype(BF16)
    count = r.count[0, 0, 0]

    def near_step(b, carry):
        source = pair_rows(r.source, b)
        target = pair_rows(r.target, b)
        live = 2 * b + (iota((1, BL), 1) >= PB).astype(jnp.int32) < count
        target = jnp.where(live, target, -1)
        atoms = iota((AP, BL), 0)
        pick_own = (atoms == source).astype(BF16)
        pick_target = (atoms == target).astype(BF16)
        r.from_own[b] = pick_own
        r.to_own[b, 0:AP, :] = pick_target
        r.to_own[b, AP : 2 * AP, :] = pick_target
        near = dot(r.own_table[...], pick_own)
        here = dot(r.own_table[CH : CH + 16, :], pick_target)
        r.near[:, span(b)] = jnp.concatenate([near[:CH], near[CH : CH + 8] - here[:8]], 0)
        return carry

    lax.fori_loop(0, STEPS, near_step, 0)


def gather(r):
    def far_step(b, carry):
        source = pair_rows(r.source, b)
        pick_ghost = (r.keys[...] == source.astype(KEY)).astype(BF16)
        r.from_ghost[b] = pick_ghost
        far = dot(r.table[...], pick_ghost)
        near = r.near[:, span(b)]
        r.feats[:, span(b)] = (near[:CH] + far[:CH]) * SCALE
        r.geom[0:3, span(b)] = (
            near[CH : CH + 3] + far[CH + 4 : CH + 7] + SIDE * far[CH + 8 : CH + 11]
        )
        return carry

    lax.fori_loop(0, STEPS, far_step, 0)


def harmonics_of(x, y, z):
    return [
        ROOT3 * x * y,
        ROOT3 * y * z,
        0.5 * (2.0 * z * z - x * x - y * y),
        ROOT3 * x * z,
        0.5 * ROOT3 * (x * x - y * y),
    ]


def radial(r):
    v = r.geom[0:3, :]
    q = v[0:1] * v[0:1] + v[1:2] * v[1:2] + v[2:3] * v[2:3]
    keep = jnp.maximum(1.0 - q / CUT, 0.0)
    envelope = keep * keep
    d_envelope = keep * (-2.0 / CUT)
    centers = iota((NRB, NP), 0).astype(F32) * (CUT / (NRB - 1))
    away = q - centers
    bump = jnp.exp(-(away * away) / CUT)
    basis = bump * envelope
    d_basis = bump * (d_envelope - (2.0 / CUT) * away * envelope)
    first = twice_across(r.first)
    z = dot(first, jnp.concatenate([stack_high_low(basis), stack_high_low(d_basis)], 1))
    h, slope = silu_parts(z[:, :NP])
    d = slope * z[:, NP:]
    second = twice_across(r.second)
    z = dot(second, jnp.concatenate([stack_high_low(h), stack_high_low(d)], 1))
    h, slope = silu_parts(z[:, :NP])
    d = slope * z[:, NP:]
    r.hidden[0] = stack_high_low(h)
    r.hidden[1] = stack_high_low(d)


def scatter(r):
    third = twice_across(r.third)
    r.moments[...] = jnp.zeros_like(r.moments)

    def step(b, carry):
        feats = r.feats[:, span(b)]
        v = r.geom[0:3, span(b)]
        z = dot(third, r.hidden[0, :, span(b)])
        d = dot(third, r.hidden[1, :, span(b)])
        ux, uy, uz = 0.5 * v[0:1], 0.5 * v[1:2], 0.5 * v[2:3]
        harmonics = [[None], [ux, uy, uz], harmonics_of(ux, uy, uz)]
        row = 0
        for order in range(3):
            part = slice(CH * order, CH * (order + 1))
            weighted = z[part] * feats
            r.radial[b, part, :] = weighted
            r.slope[b, part, :] = d[part] * feats
            for harmonic in harmonics[order]:
                term = weighted if harmonic is None else weighted * harmonic
                high, low = high_low(term)
                r.terms[row : row + CH, 0:BL] = high.astype(BF16)
                r.terms[row : row + CH, BL : 2 * BL] = low.astype(BF16)
                row += CH
        pick_target = r.to_own[b, 0:AP, :]
        twice = jnp.concatenate([pick_target, pick_target], 1)
        r.moments[...] += dot(r.terms[...], twice, NT)
        return carry

    lax.fori_loop(0, STEPS, step, 0)


def readout(r):
    def moment(i):
        return r.moments[CH * i : CH * (i + 1), :]

    squares = []
    for low, high in ((1, 4), (4, 9)):
        total = moment(low) * moment(low)
        for i in range(low + 1, high):
            total = total + moment(i) * moment(i)
        squares.append(total)
    invariants = jnp.concatenate([moment(0)] + squares, 0)
    mix = r.mix[...]
    mix_t = mix.astype(F32).T.astype(BF16)
    high, low = high_low(invariants)
    mixed = dot(mix_t, high.astype(BF16)) + dot(mix_t, low.astype(BF16))
    head = jnp.broadcast_to(r.head[...].astype(F32), (128, 128)).T
    head = jnp.concatenate([head] * 4, 1)
    h, slope = silu_parts(mixed)
    d_mixed = stack_high_low(head * slope)
    d_inv = dot(jnp.concatenate([mix, mix], 1), d_mixed)
    for i in range(9):
        order = 0 if i == 0 else (1 if i < 4 else 2)
        grad = d_inv[CH * order : CH * (order + 1)]
        if order:
            grad = 2.0 * moment(i) * grad
        high, low = high_low(grad)
        r.grads[CH * i : CH * (i + 1), 0:AP] = high.astype(BF16)
        r.grads[CH * i : CH * (i + 1), AP : 2 * AP] = low.astype(BF16)
    energy = jnp.sum(head * h, axis=0, keepdims=True)[:, :A]
    kinds = r.species[...]
    for k in range(SPECIES):
        energy = energy + jnp.where(kinds == k, r.shift[k], 0.0)
    r.out[0] = energy


def pulls(r):
    def step(b, carry):
        r.back[...] = dot(r.grads[...], r.to_own[b])
        v = r.geom[0:3, span(b)]
        along, across = [], []
        for i in range(9):
            order = 0 if i == 0 else (1 if i < 4 else 2)
            part = slice(CH * order, CH * (order + 1))
            grad = r.back[CH * i : CH * (i + 1), :]
            if order:
                along.append(jnp.sum(r.radial[b, part, :] * grad, axis=0, keepdims=True))
            across.append(jnp.sum(r.slope[b, part, :] * grad, axis=0, keepdims=True))
        x, y, z = 0.5 * v[0:1], 0.5 * v[1:2], 0.5 * v[2:3]
        ax, ay, az, b0, b1, b2, b3, b4 = along
        dq = across[0] + x * across[1] + y * across[2] + z * across[3]
        for harmonic, c in zip(harmonics_of(x, y, z), across[4:]):
            dq = dq + harmonic * c
        gx = ax + ROOT3 * (y * b0 + z * b3 + x * b4) - x * b2
        gy = ay + ROOT3 * (x * b0 + z * b1 - y * b4) - y * b2
        gz = az + ROOT3 * (y * b1 + x * b3) + 2.0 * z * b2
        px = 0.5 * gx + 2.0 * dq * v[0:1]
        py = 0.5 * gy + 2.0 * dq * v[1:2]
        pz = 0.5 * gz + 2.0 * dq * v[2:3]
        pull = jnp.concatenate([px, py, pz, jnp.zeros((5, BL), F32)], 0)
        r.pull[b] = stack_high_low(pull)
        return carry

    lax.fori_loop(0, STEPS, step, 0)


def spread(pull_ref, pick):
    total = None
    for b in range(STEPS):
        part = dot(pull_ref[b], pick(b), NT)
        total = part if total is None else total + part
    return total[:8] + total[8:]


def give_ghosts(r):
    r.ghost[...] = -spread(r.pull, lambda b: r.from_ghost[b])


def own_forces(r):
    return spread(r.pull, lambda b: r.to_own[b, 0:AP, :] - r.from_own[b])


class Refs:
    def __init__(self, names, refs):
        for name, ref in zip(names, refs, strict=True):
            setattr(self, name, ref)


LOADS = {
    "pos": ((3, A), BF16),
    "feat": ((A, CH), BF16),
    "list": ((1, G), jnp.int32),
    "source": ((NB, 1, PB), jnp.int32),
    "target": ((NB, 1, PB), jnp.int32),
    "first": ((NRB, RH), BF16),
    "second": ((RH, RH), BF16),
    "third": ((RH, 3 * CH), BF16),
    "mix": ((3 * CH, CH), BF16),
    "head": ((1, CH), BF16),
    "species": ((1, A), jnp.int32),
}
WORK = {
    "own_table": ((CH + 16, AP), BF16),
    "table": ((CH + 16, GT), BF16),
    "keys": ((GT, BL), KEY),
    "from_own": ((STEPS, AP, BL), BF16),
    "from_ghost": ((STEPS, GT, BL), BF16),
    "to_own": ((STEPS, 2 * AP, BL), BF16),
    "near": ((CH + 8, NP), F32),
    "feats": ((CH, NP), F32),
    "geom": ((8, NP), F32),
    "hidden": ((2, 2 * RH, NP), BF16),
    "radial": ((STEPS, 3 * CH, BL), F32),
    "slope": ((STEPS, 3 * CH, BL), F32),
    "terms": ((9 * CH, 2 * BL), BF16),
    "moments": ((9 * CH, AP), F32),
    "grads": ((9 * CH, 2 * AP), BF16),
    "back": ((9 * CH, BL), F32),
    "pull": ((STEPS, 16, BL), BF16),
    "ghost": ((8, GT), F32),
    "pick": ((GT, A), BF16),
    "sent": ((SENT, CH), BF16),
    "got": ((SENT, CH), BF16),
    "returned": ((26, 8, 128), F32),
}
INPUTS = ["count", "shift"] + ["hbm_" + name for name in LOADS]
NAMES = INPUTS + ["out"] + list(LOADS) + list(WORK)
NAMES += ["load_sem", "send_sem", "recv_sem", "back_send_sem", "back_recv_sem"]


def kernel(*refs):
    r = Refs(NAMES, refs)
    loads = {}
    for i, name in enumerate(LOADS):
        loads[name] = pltpu.make_async_copy(
            getattr(r, "hbm_" + name), getattr(r, name), r.load_sem.at[i]
        )
        loads[name].start()
    barrier = enter()
    for name in ("pos", "feat", "list"):
        loads.pop(name).wait()
    choose(r.pos, r.feat, r.list, r.pick, r.sent)
    pl.semaphore_wait(barrier, 26)
    copies = []
    for i, (slot, rows, row, _) in enumerate(PLACES):
        copies.append(
            pltpu.make_async_remote_copy(
                src_ref=r.sent.at[row : row + rows, :],
                dst_ref=r.got.at[row : row + rows, :],
                send_sem=r.send_sem.at[i],
                recv_sem=r.recv_sem.at[i],
                device_id=neighbour(slot, -1),
                device_id_type=MESH,
            )
        )
        copies[-1].start()
    for copy in loads.values():
        copy.wait()
    prepare(r)
    for copy in copies:
        copy.wait()
    ghost_table(r.got, r.table, r.keys)
    gather(r)
    radial(r)
    scatter(r)
    readout(r)
    pulls(r)
    give_ghosts(r)
    copies = []
    for i, (slot, rows, _, lane) in enumerate(PLACES):
        start = lane // 128 * 128
        copies.append(
            pltpu.make_async_remote_copy(
                src_ref=r.ghost.at[:, start : start + 128],
                dst_ref=r.returned.at[i],
                send_sem=r.back_send_sem.at[i],
                recv_sem=r.back_recv_sem.at[i],
                device_id=neighbour(slot, 1),
                device_id_type=MESH,
            )
        )
        copies[-1].start()
    own = own_forces(r)[:, :A]
    for copy in copies:
        copy.wait()
    tiles = [[] for _ in range(10)]
    for i, place in enumerate(PLACES):
        tiles[place[3] // 128].append(r.returned[i])
    tiles = [group_lanes(members, 128 // len(members)) for members in tiles]
    sums = dot(stack_high_low(jnp.concatenate(tiles, 1)), r.pick[...])
    total = own + sums[:8] + sums[8:]
    for axis in range(3):
        r.out[axis + 1] = total[axis : axis + 1]


def vmem():
    return pl.BlockSpec(memory_space=pltpu.VMEM)


def smem():
    return pl.BlockSpec(memory_space=pltpu.SMEM)


def shape(dims, kind=F32):
    return jax.ShapeDtypeStruct(dims, kind)


def shards(
    positions,
    features,
    species,
    species_shift,
    send_index,
    pair_target,
    pair_source,
    block_count,
    radial_first,
    radial_second,
    radial_third,
    invariant_mix,
    energy_head,
):
    both = pl.pallas_call(
        kernel,
        out_shape=shape((4, 1, A)),
        in_specs=[smem()] * 2 + [pl.BlockSpec(memory_space=pl.ANY)] * len(LOADS),
        out_specs=vmem(),
        scratch_shapes=[pltpu.VMEM(*spec) for spec in LOADS.values()]
        + [pltpu.VMEM(*spec) for spec in WORK.values()]
        + [pltpu.SemaphoreType.DMA((len(LOADS),))]
        + [pltpu.SemaphoreType.DMA((26,))] * 4,
        compiler_params=pltpu.CompilerParams(
            collective_id=0, has_side_effects=True, vmem_limit_bytes=56 * 2**20
        ),
        name="layer",
    )(
        block_count,
        species_shift,
        positions.reshape(3, A),
        jnp.swapaxes(features, 3, 4).reshape(A, CH),
        send_index.reshape(1, G),
        pair_source.reshape(NB, 1, PB),
        pair_target.reshape(NB, 1, PB),
        radial_first,
        radial_second,
        radial_third,
        invariant_mix,
        energy_head.reshape(1, CH),
        species.reshape(1, A),
    )
    return (both[0].reshape(1, 1, 1, A), both[1:].reshape(1, 1, 1, 3, A))


def solution(mesh):
    split = ("gx", "gy", "gz")
    return jax.shard_map(
        shards,
        mesh=mesh,
        in_specs=(
            P(*split, None, None),
            P(*split, None, None),
            P(*split, None),
            P(),
            P(*split, None),
            P(*split, None, None),
            P(*split, None, None),
            P(*split),
            P(),
            P(),
            P(),
            P(),
            P(),
        ),
        out_specs=(P(*split, None), P(*split, None, None)),
        check_vma=False,
    )
```

time: 57 us -> 44.2 us (0.78)
  local copies, waits for them, and re-layouts: 9.43 us -> 2.55 us
  Pallas kernels: 45.8 us -> 40.2 us
    unnamed x23 -> x1, local copies, waits for them, and re-layouts: 9.43 us -> 1.28 us
    pallas_call x3 -> x1, Pallas kernels: 45.8 us -> 40.2 us  [shards(): pl.pallas_call(kernel, out_shape=shape((4, 1, A)), in_specs=[smem()] * 2...]
    another operation x0 -> x1, local copies, waits for them, and re-layouts: none -> 1.26 us  [shards(): return (both[0].reshape(1, 1, 1, A), both[1:].reshape(1, 1, 1, 3, A))]
where the time goes in v2:
time: 44.2 us; the launch traced here: 44 us
  Pallas kernels  40.2 us (91%)
  local copies, waits for them, and re-layouts  2.55 us (6%)
  between operations  1.29 us (3%)
    pallas_call x1, Pallas kernels, shards(): pl.pallas_call(kernel, out_shape=shape((4, 1, A)), in_specs=[smem()] * 2...  40.2 us
    unnamed x1, local copies, waits for them, and re-layouts  1.28 us
    another operation x1, local copies, waits for them, and re-layouts, shards(): return (both[0].reshape(1, 1, 1, A), both[1:].reshape(1, 1, 1, 3, A))  1.26 us

profile of v2, /device:TPU:1, one launch (start us, length us, event | category | flops | bytes accessed | tf_op | source)
XLA Modules:
  0.0 44.0 jit_solution(2791849356043998580)
XLA Ops:
  1.3 40.2 %layer.1 = f32[4,1,432]{2,1,0:T(1,128)} custom-call(s32[1,1,1]{2,1,0:T(1,128)S(6)} %copy.16.refs_0_, f32[10]{0:T(128)} %refs_1_.1, bf16[3,432]{1,0:T(4,128)(2,1)} %bitcast.18, bf16[432,128]{1,0:T(8,128)(2,1)} %bitcast.15, s32[1,304]{1,0:T(1,128)} %bitcast.20, s32[10,1,128]{2,1,0:T(1,128)} %bitcast.16, s32[10,1,128]{2,1,0:T(1,128)} %bitcast.17, ...), custom_call_target="tpu_custom_call" | custom-call | tf_op jit(solution)/shard_map/layer/pallas_call | solution.py:555
  41.5 1.3 %slice_bitcast_fusion.1 = f32[1,1,1,432]{3,2,1,0:T(1,128)} fusion(f32[4,1,432]{2,1,0:T(1,128)} %layer.1), kind=kLoop, calls=%fused_computation.1 | loop fusion | bytes 3456 | tf_op jit(solution)/shard_map/reshape;squeeze | solution.py:583
  42.7 1.3 %slice_bitcast_fusion = f32[1,1,1,3,432]{4,2,3,1,0:T(1,128)} fusion(f32[4,1,432]{2,1,0:T(1,128)} %layer.1), kind=kLoop, calls=%fused_computation | loop fusion | bytes 10368

commit v3 on v2

--- a/solution.py
+++ b/solution.py
@@ -59,6 +59,17 @@
 PLACES = places()
 
 
+def far_first():
+    def way(place):
+        x, y, z = offset_of(place[0])
+        return -(4 * abs(z) + 2 * abs(y) + abs(x))
+
+    return sorted(enumerate(PLACES), key=lambda item: way(item[1]))
+
+
+ORDER = far_first()
+
+
 def dot(a, b, dims=NN):
     return lax.dot_general(a, b, dims, preferred_element_type=F32)
 
@@ -72,20 +83,23 @@
     return high, x - high
 
 
-def neighbour(slot, sign):
-    where = []
-    for axis, size, step in zip(("gx", "gy", "gz"), (4, 4, 16), offset_of(slot)):
+def neighbours():
+    steps = {}
+    for axis, size in (("gx", 4), ("gy", 4), ("gz", 16)):
         me = lax.axis_index(axis)
-        where.append(lax.rem(me + (size + sign * step), size) if step else me)
-    return tuple(where)
-
-
-def enter():
+        steps[axis] = {0: me, 1: lax.rem(me + 1, size), -1: lax.rem(me + size - 1, size)}
+
+    def at(slot, sign):
+        offset = offset_of(slot)
+        return tuple(steps[axis][sign * o] for axis, o in zip(("gx", "gy", "gz"), offset))
+
+    return at
+
+
+def enter(at):
     barrier = pltpu.get_barrier_semaphore()
-    for slot, *_ in PLACES:
-        pl.semaphore_signal(
-            barrier, inc=1, device_id=neighbour(slot, 1), device_id_type=MESH
-        )
+    for _, (slot, *_) in ORDER:
+        pl.semaphore_signal(barrier, inc=1, device_id=at(slot, 1), device_id_type=MESH)
     return barrier
 
 
@@ -243,12 +257,19 @@
         r.from_own[b] = pick_own
         r.to_own[b, 0:AP, :] = pick_target
         r.to_own[b, AP : 2 * AP, :] = pick_target
+        across = iota((PB, AP), 1)
+        for half in range(2):
+            part = jnp.broadcast_to(target[:, PB * half : PB * (half + 1)], (PB, PB))
+            column = part.astype(F32).T.astype(jnp.int32)
+            pick = (across == jnp.concatenate([column] * 4, 1)).astype(BF16)
+            r.by_pair[512 * b + PB * half : 512 * b + PB * (half + 1), :] = pick
+            r.by_pair[512 * b + BL + PB * half : 512 * b + BL + PB * (half + 1), :] = pick
         near = dot(r.own_table[...], pick_own)
         here = dot(r.own_table[CH : CH + 16, :], pick_target)
         r.near[:, span(b)] = jnp.concatenate([near[:CH], near[CH : CH + 8] - here[:8]], 0)
         return carry
 
-    lax.fori_loop(0, STEPS, near_step, 0)
+    for b in range(STEPS): near_step(b, 0)
 
 
 def gather(r):
@@ -264,7 +285,7 @@
         )
         return carry
 
-    lax.fori_loop(0, STEPS, far_step, 0)
+    lax.fori_loop(0, STEPS, far_step, 0, unroll=True)
 
 
 def harmonics_of(x, y, z):
@@ -300,35 +321,32 @@
     r.hidden[1] = stack_high_low(d)
 
 
+CHUNKS = ((0, 4), (4, 9))
+
+
 def scatter(r):
     third = twice_across(r.third)
-    r.moments[...] = jnp.zeros_like(r.moments)
-
-    def step(b, carry):
-        feats = r.feats[:, span(b)]
-        v = r.geom[0:3, span(b)]
-        z = dot(third, r.hidden[0, :, span(b)])
-        d = dot(third, r.hidden[1, :, span(b)])
-        ux, uy, uz = 0.5 * v[0:1], 0.5 * v[1:2], 0.5 * v[2:3]
-        harmonics = [[None], [ux, uy, uz], harmonics_of(ux, uy, uz)]
-        row = 0
-        for order in range(3):
-            part = slice(CH * order, CH * (order + 1))
-            weighted = z[part] * feats
-            r.radial[b, part, :] = weighted
-            r.slope[b, part, :] = d[part] * feats
-            for harmonic in harmonics[order]:
-                term = weighted if harmonic is None else weighted * harmonic
+    v = r.geom[0:3, :]
+    ux, uy, uz = 0.5 * v[0:1], 0.5 * v[1:2], 0.5 * v[2:3]
+    harmonics = [None, ux, uy, uz] + harmonics_of(ux, uy, uz)
+    for first, last in CHUNKS:
+        for b in range(STEPS):
+            lanes = slice(BL * b, BL * (b + 1))
+            for i in range(first, last):
+                order = 0 if i == 0 else (1 if i < 4 else 2)
+                part = slice(CH * order, CH * (order + 1))
+                if i in (0, 1, 4):
+                    z = dot(third[part], r.hidden[0, :, lanes])
+                    r.radial[b, part, :] = z * r.feats[:, lanes]
+                term = r.radial[b, part, :]
+                if i:
+                    term = term * harmonics[i][:, lanes]
                 high, low = high_low(term)
-                r.terms[row : row + CH, 0:BL] = high.astype(BF16)
-                r.terms[row : row + CH, BL : 2 * BL] = low.astype(BF16)
-                row += CH
-        pick_target = r.to_own[b, 0:AP, :]
-        twice = jnp.concatenate([pick_target, pick_target], 1)
-        r.moments[...] += dot(r.terms[...], twice, NT)
-        return carry
-
-    lax.fori_loop(0, STEPS, step, 0)
+                row = CH * i
+                r.terms[row : row + CH, 512 * b : 512 * b + BL] = high.astype(BF16)
+                r.terms[row : row + CH, 512 * b + BL : 512 * b + 512] = low.astype(BF16)
+        rows = slice(CH * first, CH * last)
+        r.moments[rows, :] = dot(r.terms[rows, :], r.by_pair[...])
 
 
 def readout(r):
@@ -367,17 +385,21 @@
 
 
 def pulls(r):
+    third = twice_across(r.third)
+
     def step(b, carry):
-        r.back[...] = dot(r.grads[...], r.to_own[b])
+        d = dot(third, r.hidden[1, :, span(b)])
+        r.back[b] = dot(r.grads[...], r.to_own[b])
         v = r.geom[0:3, span(b)]
         along, across = [], []
         for i in range(9):
             order = 0 if i == 0 else (1 if i < 4 else 2)
             part = slice(CH * order, CH * (order + 1))
-            grad = r.back[CH * i : CH * (i + 1), :]
+            grad = r.back[b, CH * i : CH * (i + 1), :]
             if order:
                 along.append(jnp.sum(r.radial[b, part, :] * grad, axis=0, keepdims=True))
-            across.append(jnp.sum(r.slope[b, part, :] * grad, axis=0, keepdims=True))
+            slope = d[part] * r.feats[:, span(b)]
+            across.append(jnp.sum(slope * grad, axis=0, keepdims=True))
         x, y, z = 0.5 * v[0:1], 0.5 * v[1:2], 0.5 * v[2:3]
         ax, ay, az, b0, b1, b2, b3, b4 = along
         dq = across[0] + x * across[1] + y * across[2] + z * across[3]
@@ -393,7 +415,7 @@
         r.pull[b] = stack_high_low(pull)
         return carry
 
-    lax.fori_loop(0, STEPS, step, 0)
+    for b in range(STEPS): step(b, 0)
 
 
 def spread(pull_ref, pick):
@@ -430,6 +452,8 @@
     "mix": ((3 * CH, CH), BF16),
     "head": ((1, CH), BF16),
     "species": ((1, A), jnp.int32),
+    "count": ((1, 1, 1), jnp.int32),
+    "shift": ((SPECIES,), F32),
 }
 WORK = {
     "own_table": ((CH + 16, AP), BF16),
@@ -438,16 +462,16 @@
     "from_own": ((STEPS, AP, BL), BF16),
     "from_ghost": ((STEPS, GT, BL), BF16),
     "to_own": ((STEPS, 2 * AP, BL), BF16),
+    "by_pair": ((STEPS * 2 * BL, AP), BF16),
     "near": ((CH + 8, NP), F32),
     "feats": ((CH, NP), F32),
     "geom": ((8, NP), F32),
     "hidden": ((2, 2 * RH, NP), BF16),
     "radial": ((STEPS, 3 * CH, BL), F32),
-    "slope": ((STEPS, 3 * CH, BL), F32),
-    "terms": ((9 * CH, 2 * BL), BF16),
+    "terms": ((9 * CH, STEPS * 2 * BL), BF16),
     "moments": ((9 * CH, AP), F32),
     "grads": ((9 * CH, 2 * AP), BF16),
-    "back": ((9 * CH, BL), F32),
+    "back": ((STEPS, 9 * CH, BL), F32),
     "pull": ((STEPS, 16, BL), BF16),
     "ghost": ((8, GT), F32),
     "pick": ((GT, A), BF16),
@@ -455,33 +479,34 @@
     "got": ((SENT, CH), BF16),
     "returned": ((26, 8, 128), F32),
 }
-INPUTS = ["count", "shift"] + ["hbm_" + name for name in LOADS]
+INPUTS = ["hbm_" + name for name in LOADS]
 NAMES = INPUTS + ["out"] + list(LOADS) + list(WORK)
 NAMES += ["load_sem", "send_sem", "recv_sem", "back_send_sem", "back_recv_sem"]
 
 
 def kernel(*refs):
     r = Refs(NAMES, refs)
+    at = neighbours()
+    barrier = enter(at)
     loads = {}
     for i, name in enumerate(LOADS):
         loads[name] = pltpu.make_async_copy(
             getattr(r, "hbm_" + name), getattr(r, name), r.load_sem.at[i]
         )
         loads[name].start()
-    barrier = enter()
     for name in ("pos", "feat", "list"):
         loads.pop(name).wait()
     choose(r.pos, r.feat, r.list, r.pick, r.sent)
     pl.semaphore_wait(barrier, 26)
     copies = []
-    for i, (slot, rows, row, _) in enumerate(PLACES):
+    for i, (slot, rows, row, _) in ORDER:
         copies.append(
             pltpu.make_async_remote_copy(
                 src_ref=r.sent.at[row : row + rows, :],
                 dst_ref=r.got.at[row : row + rows, :],
                 send_sem=r.send_sem.at[i],
                 recv_sem=r.recv_sem.at[i],
-                device_id=neighbour(slot, -1),
+                device_id=at(slot, -1),
                 device_id_type=MESH,
             )
         )
@@ -490,7 +515,7 @@
         copy.wait()
     prepare(r)
     for copy in copies:
-        copy.wait()
+        copy.wait_recv()
     ghost_table(r.got, r.table, r.keys)
     gather(r)
     radial(r)
@@ -498,23 +523,25 @@
     readout(r)
     pulls(r)
     give_ghosts(r)
-    copies = []
-    for i, (slot, rows, _, lane) in enumerate(PLACES):
+    returns = []
+    for i, (slot, rows, _, lane) in ORDER:
         start = lane // 128 * 128
-        copies.append(
+        returns.append(
             pltpu.make_async_remote_copy(
                 src_ref=r.ghost.at[:, start : start + 128],
                 dst_ref=r.returned.at[i],
                 send_sem=r.back_send_sem.at[i],
                 recv_sem=r.back_recv_sem.at[i],
-                device_id=neighbour(slot, 1),
+                device_id=at(slot, 1),
                 device_id_type=MESH,
             )
         )
-        copies[-1].start()
+        returns[-1].start()
     own = own_forces(r)[:, :A]
     for copy in copies:
-        copy.wait()
+        copy.wait_send()
+    for copy in returns:
+        copy.wait_recv()
     tiles = [[] for _ in range(10)]
     for i, place in enumerate(PLACES):
         tiles[place[3] // 128].append(r.returned[i])
@@ -523,14 +550,21 @@
     total = own + sums[:8] + sums[8:]
     for axis in range(3):
         r.out[axis + 1] = total[axis : axis + 1]
+    for copy in returns:
+        copy.wait_send()
+
+
+def split_kernel(both_ref, energy_ref, force_ref, sem):
+    first = pltpu.make_async_copy(both_ref.at[0:1], energy_ref, sem.at[0])
+    second = pltpu.make_async_copy(both_ref.at[1:4], force_ref, sem.at[1])
+    first.start()
+    second.start()
+    first.wait()
+    second.wait()
 
 
 def vmem():
     return pl.BlockSpec(memory_space=pltpu.VMEM)
-
-
-def smem():
-    return pl.BlockSpec(memory_space=pltpu.SMEM)
 
 
 def shape(dims, kind=F32):
@@ -555,9 +589,12 @@
     both = pl.pallas_call(
         kernel,
         out_shape=shape((4, 1, A)),
-        in_specs=[smem()] * 2 + [pl.BlockSpec(memory_space=pl.ANY)] * len(LOADS),
+        in_specs=[pl.BlockSpec(memory_space=pl.ANY)] * len(LOADS),
         out_specs=vmem(),
-        scratch_shapes=[pltpu.VMEM(*spec) for spec in LOADS.values()]
+        scratch_shapes=[
+            (pltpu.SMEM if name in ("count", "shift") else pltpu.VMEM)(*spec)
+            for name, spec in LOADS.items()
+        ]
         + [pltpu.VMEM(*spec) for spec in WORK.values()]
         + [pltpu.SemaphoreType.DMA((len(LOADS),))]
         + [pltpu.SemaphoreType.DMA((26,))] * 4,
@@ -566,8 +603,6 @@
         ),
         name="layer",
     )(
-        block_count,
-        species_shift,
         positions.reshape(3, A),
         jnp.swapaxes(features, 3, 4).reshape(A, CH),
         send_index.reshape(1, G),
@@ -579,8 +614,18 @@
         invariant_mix,
         energy_head.reshape(1, CH),
         species.reshape(1, A),
+        block_count,
+        species_shift,
     )
-    return (both[0].reshape(1, 1, 1, A), both[1:].reshape(1, 1, 1, 3, A))
+    energies, forces = pl.pallas_call(
+        split_kernel,
+        out_shape=(shape((1, 1, A)), shape((3, 1, A))),
+        in_specs=[pl.BlockSpec(memory_space=pl.ANY)],
+        out_specs=(pl.BlockSpec(memory_space=pl.ANY),) * 2,
+        scratch_shapes=[pltpu.SemaphoreType.DMA((2,))],
+        name="split",
+    )(both)
+    return (energies.reshape(1, 1, 1, A), forces.reshape(1, 1, 1, 3, A))
 
 
 def solution(mesh):

time: 44.2 us -> 38.9 us (0.88)
  Pallas kernels: 40.2 us -> 37.5 us
  local copies, waits for them, and re-layouts: 2.55 us -> 0 us
    pallas_call x1 -> x2, Pallas kernels: 40.2 us -> 37.5 us  [the longest x1 36.1 us: shards(): pl.pallas_call(kernel, out_shape=shape((4, 1, A)), in_specs=[pl.BlockSpec...]
    unnamed x1 -> x0, local copies, waits for them, and re-layouts: 1.28 us -> none
    another operation x1 -> x0, local copies, waits for them, and re-layouts: 1.26 us -> none  [shards(): return (both[0].reshape(1, 1, 1, A), both[1:].reshape(1, 1, 1, 3, A))]
where the time goes in v3:
time: 38.9 us; the launch traced here: 38.8 us
  Pallas kernels  37.5 us (96%)
  between operations  1.29 us (3%)
    pallas_call x1, Pallas kernels, shards(): pl.pallas_call(kernel, out_shape=shape((4, 1, A)), in_specs=[pl.BlockSpec...  36.1 us
    pallas_call x1, Pallas kernels, shards(): pl.pallas_call(split_kernel, out_shape=(shape((1, 1, A)), shape((3, 1, A)...  1.37 us

profile of v3, /device:TPU:1, one launch (start us, length us, event | category | flops | bytes accessed | tf_op | source)
XLA Modules:
  0.0 38.8 jit_solution(12963292726886348072)
XLA Ops:
  1.3 36.1 %layer.1.both_ref = f32[4,1,432]{2,1,0:T(1,128)} custom-call(bf16[3,432]{1,0:T(4,128)(2,1)} %bitcast.16, bf16[432,128]{1,0:T(8,128)(2,1)} %bitcast.13, s32[1,304]{1,0:T(1,128)} %bitcast.18, s32[10,1,128]{2,1,0:T(1,128)} %bitcast.14, s32[10,1,128]{2,1,0:T(1,128)} %bitcast.15, bf16[8,64]{1,0:T(8,128)(2,1)} %refs_5_.1, bf16[64,64]{1,0:T(8,128)(2,1)} %refs_6_.1, ...), custom_call_target="tpu_custom_call" | custom-call | tf_op jit(solution)/shard_map/layer/pallas_call | solution.py:589
  37.4 1.4 %split.1 = (f32[1,1,432]{2,1,0:T(1,128)}, f32[3,1,432]{2,1,0:T(1,128)}) custom-call(f32[4,1,432]{2,1,0:T(1,128)} %layer.1.both_ref), custom_call_target="tpu_custom_call" | custom-call | tf_op jit(solution)/shard_map/split/pallas_call | solution.py:620

commit v4 on v3

--- a/solution.py
+++ b/solution.py
@@ -32,7 +32,6 @@
 F32 = jnp.float32
 BF16 = jnp.bfloat16
 MESH = pl.DeviceIdType.MESH
-KEY = jnp.int32
 NN = (((1,), (0,)), ((), ()))
 NT = (((1,), (1,)), ((), ()))
 
@@ -42,21 +41,29 @@
 
 
 def places():
-    by_kind = {1: [], 2: [], 3: []}
-    for slot in range(27):
-        if slot != 13:
-            by_kind[sum(abs(c) for c in offset_of(slot))].append(slot)
     out = []
-    for i, slot in enumerate(by_kind[1]):
-        out.append((slot, 96, 96 * i, 128 * i))
-    for i, slot in enumerate(by_kind[2]):
-        out.append((slot, 32, 576 + 32 * i, 768 + 32 * i))
-    for i, slot in enumerate(by_kind[3]):
-        out.append((slot, 16, 960 + 16 * i, 1152 + 16 * i))
+    row, lane = 0, 0
+    for far in (False, True):
+        for kind, rows, lanes in ((1, 96, 128), (2, 32, 32), (3, 16, 16)):
+            for slot in range(27):
+                offset = offset_of(slot)
+                if sum(abs(c) for c in offset) == kind and (offset[2] != 0) == far:
+                    out.append((slot, rows, row, lane))
+                    row, lane = row + rows, lane + lanes
     return out
 
 
 PLACES = places()
+HALF = GT // 2
+NEAR, FAR = 0, 1
+
+
+def tiles_of(half):
+    tiles = {}
+    for i, place in enumerate(PLACES):
+        if place[3] // HALF == half:
+            tiles.setdefault(place[3] // 128, []).append((i, place))
+    return tiles
 
 
 def far_first():
@@ -103,7 +110,7 @@
     return barrier
 
 
-def choose(pos_ref, feat_ref, list_ref, pick_ref, send_ref):
+def choose(pos_ref, feat_ref, list_ref, pick_ref, send_ref, send):
     pos = pos_ref[...].astype(F32)
     entry = (iota((A, G), 0) == list_ref[...]).astype(BF16)
     ids = iota((8, G), 1).astype(F32)
@@ -139,30 +146,26 @@
         count[:32] - 1.0,
         jnp.where(closed > 0.0, total + count[32:] - 1.0, -1.0),
     )
-    for slot, rows, _, lane in PLACES:
-        tall = 128 if rows == 96 else rows
-        step = iota((tall, A), 0)
-        step = jnp.where(step < rows - 4, step, -2).astype(F32)
-        pick_ref[lane : lane + tall, :] = (step == rank[slot : slot + 1]).astype(BF16)
     meta = jnp.concatenate([jnp.zeros((4, A), F32), pos, code[0:1]], 0).astype(BF16)
     feat = feat_ref[...]
-    for slot, rows, row, lane in PLACES:
-        if rows == 96:
-            block = dot(pick_ref[lane : lane + 96, :], feat)
-            told = dot(meta, pick_ref[lane : lane + 128, :], NT)
-            out = jnp.concatenate([block[:88], block[88:96] + told], 0)
-            send_ref[row : row + 96, :] = out.astype(BF16)
-    for group in range(4):
-        start = 768 + 128 * group
-        rows = 32 if group < 3 else 16
-        block = dot(pick_ref[start : start + 128, :], feat)
-        told = dot(meta, pick_ref[start : start + 128, :], NT)
-        pieces = []
-        for i in range(128 // rows):
-            pieces.append(block[rows * i : rows * i + rows - 8])
-            pieces.append(block[rows * i + rows - 8 : rows * (i + 1)] + told)
-        row = 576 + 128 * group
-        send_ref[row : row + 128, :] = jnp.concatenate(pieces, 0).astype(BF16)
+    for half in (FAR, NEAR):
+        for t, members in tiles_of(half).items():
+            tile = slice(128 * t, 128 * (t + 1))
+            rows = members[0][1][1]
+            for _, (slot, _, _, lane) in members:
+                tall = 128 if rows == 96 else rows
+                step = iota((tall, A), 0)
+                step = jnp.where(step < rows - 4, step, -2).astype(F32)
+                pick_ref[lane : lane + tall, :] = (step == rank[slot : slot + 1]).astype(BF16)
+            block = dot(pick_ref[tile, :], feat)
+            told = dot(meta, pick_ref[tile, :], NT)
+            pieces = []
+            for i in range(len(members)):
+                pieces.append(block[rows * i : rows * i + rows - 8])
+                pieces.append(block[rows * i + rows - 8 : rows * (i + 1)] + told)
+            row = members[0][1][2]
+            send_ref[row : row + rows * len(members), :] = jnp.concatenate(pieces, 0).astype(BF16)
+        send(half)
 
 
 def group_lanes(tiles, width):
@@ -173,11 +176,9 @@
     return out
 
 
-def ghost_table(got_ref, table_ref, key_ref):
-    tiles = [[] for _ in range(10)]
-    for place in PLACES:
-        tiles[place[3] // 128].append(place)
-    for t, members in enumerate(tiles):
+def ghost_table(got_ref, table_ref, key_ref, half):
+    for t, members in tiles_of(half).items():
+        members = [place for _, place in members]
         width = 128 // len(members)
         row, rows = members[0][2], members[0][1]
         if rows == 96:
@@ -196,9 +197,9 @@
             o = offset_of(slot)
             offs.append(
                 jnp.where(
-                    sub == 0,
+                    sub == 4,
                     float(o[0]),
-                    jnp.where(sub == 1, float(o[1]), jnp.where(sub == 2, float(o[2]), 0.0)),
+                    jnp.where(sub == 5, float(o[1]), jnp.where(sub == 6, float(o[2]), 0.0)),
                 )
             )
         offs = group_lanes(offs, width)
@@ -211,7 +212,7 @@
         code = told[7:8]
         index = jnp.where(code < 0.0, code + MID, code + (MID - 1.0)) + base[0:1]
         key = jnp.where(code == 0.0, -5.0, index)
-        column = jnp.broadcast_to(key, (128, 128)).T.astype(KEY)
+        column = jnp.broadcast_to(key, (128, 128)).T.astype(jnp.int32)
         key_ref[128 * t : 128 * (t + 1), :] = jnp.concatenate([column, column], 1)
 
 
@@ -226,7 +227,7 @@
 
 
 def span(b):
-    return pl.ds(pl.multiple_of(b * BL, BL), BL)
+    return slice(BL * b, BL * (b + 1))
 
 
 def pair_rows(ref, b):
@@ -242,11 +243,12 @@
     r.own_table[...] = jnp.zeros_like(r.own_table)
     feat = r.feat[...].astype(F32).T
     r.own_table[0:CH, 0:A] = feat.astype(BF16)
-    pos = jnp.concatenate([r.pos[...].astype(F32), jnp.zeros((13, A), F32)], 0)
+    none = jnp.zeros((4, A), F32)
+    pos = jnp.concatenate([none, r.pos[...].astype(F32), none, none, none[:1]], 0)
     r.own_table[CH : CH + 16, 0:A] = pos.astype(BF16)
     count = r.count[0, 0, 0]
 
-    def near_step(b, carry):
+    for b in range(STEPS):
         source = pair_rows(r.source, b)
         target = pair_rows(r.target, b)
         live = 2 * b + (iota((1, BL), 1) >= PB).astype(jnp.int32) < count
@@ -267,25 +269,23 @@
         near = dot(r.own_table[...], pick_own)
         here = dot(r.own_table[CH : CH + 16, :], pick_target)
         r.near[:, span(b)] = jnp.concatenate([near[:CH], near[CH : CH + 8] - here[:8]], 0)
-        return carry
-
-    for b in range(STEPS): near_step(b, 0)
-
-
-def gather(r):
-    def far_step(b, carry):
-        source = pair_rows(r.source, b)
-        pick_ghost = (r.keys[...] == source.astype(KEY)).astype(BF16)
-        r.from_ghost[b] = pick_ghost
-        far = dot(r.table[...], pick_ghost)
-        near = r.near[:, span(b)]
-        r.feats[:, span(b)] = (near[:CH] + far[:CH]) * SCALE
-        r.geom[0:3, span(b)] = (
-            near[CH : CH + 3] + far[CH + 4 : CH + 7] + SIDE * far[CH + 8 : CH + 11]
-        )
-        return carry
-
-    lax.fori_loop(0, STEPS, far_step, 0, unroll=True)
+
+
+def gather(r, half):
+    rows = slice(HALF * half, HALF * (half + 1))
+    for b in range(STEPS):
+        lanes = span(b)
+        pick_ghost = (r.keys[rows, :] == pair_rows(r.source, b)).astype(BF16)
+        r.from_ghost[b, rows, :] = pick_ghost
+        found = dot(r.table[:, rows], pick_ghost)
+        feats = r.near[:CH, lanes] + found[:CH]
+        place = r.near[CH : CH + 8, lanes] + found[CH : CH + 8] + SIDE * found[CH + 8 : CH + 16]
+        if half == NEAR:
+            r.near[:CH, lanes] = feats
+            r.near[CH : CH + 8, lanes] = place
+        else:
+            r.feats[:, lanes] = feats * SCALE
+            r.geom[:, lanes] = place
 
 
 def harmonics_of(x, y, z):
@@ -299,7 +299,7 @@
 
 
 def radial(r):
-    v = r.geom[0:3, :]
+    v = r.geom[4:7, :]
     q = v[0:1] * v[0:1] + v[1:2] * v[1:2] + v[2:3] * v[2:3]
     keep = jnp.maximum(1.0 - q / CUT, 0.0)
     envelope = keep * keep
@@ -326,7 +326,7 @@
 
 def scatter(r):
     third = twice_across(r.third)
-    v = r.geom[0:3, :]
+    v = r.geom[4:7, :]
     ux, uy, uz = 0.5 * v[0:1], 0.5 * v[1:2], 0.5 * v[2:3]
     harmonics = [None, ux, uy, uz] + harmonics_of(ux, uy, uz)
     for first, last in CHUNKS:
@@ -338,6 +338,8 @@
                 if i in (0, 1, 4):
                     z = dot(third[part], r.hidden[0, :, lanes])
                     r.radial[b, part, :] = z * r.feats[:, lanes]
+                    z = dot(third[part], r.hidden[1, :, lanes])
+                    r.slope[b, part, :] = z * r.feats[:, lanes]
                 term = r.radial[b, part, :]
                 if i:
                     term = term * harmonics[i][:, lanes]
@@ -385,12 +387,9 @@
 
 
 def pulls(r):
-    third = twice_across(r.third)
-
-    def step(b, carry):
-        d = dot(third, r.hidden[1, :, span(b)])
+    for b in range(STEPS):
         r.back[b] = dot(r.grads[...], r.to_own[b])
-        v = r.geom[0:3, span(b)]
+        v = r.geom[4:7, span(b)]
         along, across = [], []
         for i in range(9):
             order = 0 if i == 0 else (1 if i < 4 else 2)
@@ -398,7 +397,7 @@
             grad = r.back[b, CH * i : CH * (i + 1), :]
             if order:
                 along.append(jnp.sum(r.radial[b, part, :] * grad, axis=0, keepdims=True))
-            slope = d[part] * r.feats[:, span(b)]
+            slope = r.slope[b, part, :]
             across.append(jnp.sum(slope * grad, axis=0, keepdims=True))
         x, y, z = 0.5 * v[0:1], 0.5 * v[1:2], 0.5 * v[2:3]
         ax, ay, az, b0, b1, b2, b3, b4 = along
@@ -413,9 +412,6 @@
         pz = 0.5 * gz + 2.0 * dq * v[2:3]
         pull = jnp.concatenate([px, py, pz, jnp.zeros((5, BL), F32)], 0)
         r.pull[b] = stack_high_low(pull)
-        return carry
-
-    for b in range(STEPS): step(b, 0)
 
 
 def spread(pull_ref, pick):
@@ -426,8 +422,9 @@
     return total[:8] + total[8:]
 
 
-def give_ghosts(r):
-    r.ghost[...] = -spread(r.pull, lambda b: r.from_ghost[b])
+def give_ghosts(r, half):
+    rows = slice(HALF * half, HALF * (half + 1))
+    r.ghost[:, rows] = -spread(r.pull, lambda b: r.from_ghost[b, rows, :])
 
 
 def own_forces(r):
@@ -458,7 +455,7 @@
 WORK = {
     "own_table": ((CH + 16, AP), BF16),
     "table": ((CH + 16, GT), BF16),
-    "keys": ((GT, BL), KEY),
+    "keys": ((GT, BL), jnp.int32),
     "from_own": ((STEPS, AP, BL), BF16),
     "from_ghost": ((STEPS, GT, BL), BF16),
     "to_own": ((STEPS, 2 * AP, BL), BF16),
@@ -468,6 +465,7 @@
     "geom": ((8, NP), F32),
     "hidden": ((2, 2 * RH, NP), BF16),
     "radial": ((STEPS, 3 * CH, BL), F32),
+    "slope": ((STEPS, 3 * CH, BL), F32),
     "terms": ((9 * CH, STEPS * 2 * BL), BF16),
     "moments": ((9 * CH, AP), F32),
     "grads": ((9 * CH, 2 * AP), BF16),
@@ -496,12 +494,15 @@
         loads[name].start()
     for name in ("pos", "feat", "list"):
         loads.pop(name).wait()
-    choose(r.pos, r.feat, r.list, r.pick, r.sent)
-    pl.semaphore_wait(barrier, 26)
-    copies = []
-    for i, (slot, rows, row, _) in ORDER:
-        copies.append(
-            pltpu.make_async_remote_copy(
+    copies = {}
+
+    def send(half):
+        if half == FAR:
+            pl.semaphore_wait(barrier, 26)
+        for i, (slot, rows, row, lane) in ORDER:
+            if lane // HALF != half:
+                continue
+            copies[i] = pltpu.make_async_remote_copy(
                 src_ref=r.sent.at[row : row + rows, :],
                 dst_ref=r.got.at[row : row + rows, :],
                 send_sem=r.send_sem.at[i],
@@ -509,25 +510,30 @@
                 device_id=at(slot, -1),
                 device_id_type=MESH,
             )
-        )
-        copies[-1].start()
+            copies[i].start()
+
+    choose(r.pos, r.feat, r.list, r.pick, r.sent, send)
     for copy in loads.values():
         copy.wait()
     prepare(r)
-    for copy in copies:
-        copy.wait_recv()
-    ghost_table(r.got, r.table, r.keys)
-    gather(r)
+    for half in (NEAR, FAR):
+        for members in tiles_of(half).values():
+            for i, _ in members:
+                copies[i].wait_recv()
+        ghost_table(r.got, r.table, r.keys, half)
+        gather(r, half)
     radial(r)
     scatter(r)
     readout(r)
     pulls(r)
-    give_ghosts(r)
-    returns = []
-    for i, (slot, rows, _, lane) in ORDER:
-        start = lane // 128 * 128
-        returns.append(
-            pltpu.make_async_remote_copy(
+    returns = {}
+    for half in (FAR, NEAR):
+        give_ghosts(r, half)
+        for i, (slot, rows, _, lane) in ORDER:
+            if lane // HALF != half:
+                continue
+            start = lane // 128 * 128
+            returns[i] = pltpu.make_async_remote_copy(
                 src_ref=r.ghost.at[:, start : start + 128],
                 dst_ref=r.returned.at[i],
                 send_sem=r.back_send_sem.at[i],
@@ -535,22 +541,23 @@
                 device_id=at(slot, 1),
                 device_id_type=MESH,
             )
-        )
-        returns[-1].start()
-    own = own_forces(r)[:, :A]
-    for copy in copies:
+            returns[i].start()
+    total = own_forces(r)[:, :A]
+    for copy in copies.values():
         copy.wait_send()
-    for copy in returns:
-        copy.wait_recv()
-    tiles = [[] for _ in range(10)]
-    for i, place in enumerate(PLACES):
-        tiles[place[3] // 128].append(r.returned[i])
-    tiles = [group_lanes(members, 128 // len(members)) for members in tiles]
-    sums = dot(stack_high_low(jnp.concatenate(tiles, 1)), r.pick[...])
-    total = own + sums[:8] + sums[8:]
+    for half in (NEAR, FAR):
+        tiles = []
+        for members in tiles_of(half).values():
+            for i, _ in members:
+                returns[i].wait_recv()
+            got = [r.returned[i] for i, _ in members]
+            tiles.append(group_lanes(got, 128 // len(members)))
+        got = stack_high_low(jnp.concatenate(tiles, 1))
+        sums = dot(got, r.pick[HALF * half : HALF * (half + 1), :])
+        total = total + sums[:8] + sums[8:]
     for axis in range(3):
         r.out[axis + 1] = total[axis : axis + 1]
-    for copy in returns:
+    for copy in returns.values():
         copy.wait_send()
 
 
@@ -588,7 +595,7 @@
 ):
     both = pl.pallas_call(
         kernel,
-        out_shape=shape((4, 1, A)),
+        out_shape=pltpu.VMEM((4, 1, A), F32),
         in_specs=[pl.BlockSpec(memory_space=pl.ANY)] * len(LOADS),
         out_specs=vmem(),
         scratch_shapes=[
@@ -620,9 +627,10 @@
     energies, forces = pl.pallas_call(
         split_kernel,
         out_shape=(shape((1, 1, A)), shape((3, 1, A))),
-        in_specs=[pl.BlockSpec(memory_space=pl.ANY)],
+        in_specs=[vmem()],
         out_specs=(pl.BlockSpec(memory_space=pl.ANY),) * 2,
         scratch_shapes=[pltpu.SemaphoreType.DMA((2,))],
+        compiler_params=pltpu.CompilerParams(vmem_limit_bytes=2**20),
         name="split",
     )(both)
     return (energies.reshape(1, 1, 1, A), forces.reshape(1, 1, 1, 3, A))

time: 38.9 us -> 37.3 us (0.959)
  Pallas kernels: 37.5 us -> 35.9 us
    pallas_call x1, Pallas kernels: 36.1 us -> 35.3 us  [shards(): pl.pallas_call(kernel, out_shape=pltpu.VMEM((4, 1, A), F32), in_specs=[pl...]
    pallas_call x1, Pallas kernels: 1.37 us -> 0.62 us  [shards(): pl.pallas_call(split_kernel, out_shape=(shape((1, 1, A)), shape((3, 1, A)...]
where the time goes in v4:
time: 37.3 us; the launch traced here: 37.2 us
  Pallas kernels  35.9 us (96%)
  between operations  1.29 us (3%)
    pallas_call x1, Pallas kernels, shards(): pl.pallas_call(kernel, out_shape=pltpu.VMEM((4, 1, A), F32), in_specs=[pl...  35.3 us

profile of v4, /device:TPU:1, one launch (start us, length us, event | category | flops | bytes accessed | tf_op | source)
XLA Modules:
  0.0 37.2 jit_solution(4448255532327733991)
XLA Ops:
  1.3 35.3 %layer.1.both_ref = f32[4,1,432]{2,1,0:T(1,128)S(1)} custom-call(bf16[3,432]{1,0:T(4,128)(2,1)} %bitcast.16, bf16[432,128]{1,0:T(8,128)(2,1)} %bitcast.13, s32[1,304]{1,0:T(1,128)} %bitcast.18, s32[10,1,128]{2,1,0:T(1,128)} %bitcast.14, s32[10,1,128]{2,1,0:T(1,128)} %bitcast.15, bf16[8,64]{1,0:T(8,128)(2,1)} %refs_5_.1, bf16[64,64]{1,0:T(8,128)(2,1)} %refs_6_.1, ...), custom_call_target="tpu_custom_call" | custom-call | tf_op jit(solution)/shard_map/layer/pallas_call | solution.py:596
  36.6 0.6 %split.1 = (f32[1,1,432]{2,1,0:T(1,128)}, f32[3,1,432]{2,1,0:T(1,128)}) custom-call(f32[4,1,432]{2,1,0:T(1,128)S(1)} %layer.1.both_ref), custom_call_target="tpu_custom_call" | custom-call | tf_op jit(solution)/shard_map/split/pallas_call | solution.py:627

commit v5 on v4

--- a/solution.py
+++ b/solution.py
@@ -110,7 +110,7 @@
     return barrier
 
 
-def choose(pos_ref, feat_ref, list_ref, pick_ref, send_ref, send):
+def choose(pos_ref, feat_ref, list_ref, upper_ref, pick_ref, send_ref, send):
     pos = pos_ref[...].astype(F32)
     entry = (iota((A, G), 0) == list_ref[...]).astype(BF16)
     ids = iota((8, G), 1).astype(F32)
@@ -138,8 +138,7 @@
             jnp.where(index == 2, (x <= CELL).astype(F32), one),
         )
     both = jnp.concatenate([strict, closed - strict], 0)
-    upper = (iota((A, A), 0) <= iota((A, A), 1)).astype(BF16)
-    count = dot(both.astype(BF16), upper)
+    count = dot(both.astype(BF16), upper_ref[...])
     total = count[:32, A - 1 : A]
     rank = jnp.where(
         strict > 0.0,
@@ -246,6 +245,19 @@
     none = jnp.zeros((4, A), F32)
     pos = jnp.concatenate([none, r.pos[...].astype(F32), none, none, none[:1]], 0)
     r.own_table[CH : CH + 16, 0:A] = pos.astype(BF16)
+    r.first_t[...] = twice_across(r.first)
+    r.second_t[...] = twice_across(r.second)
+    r.third_t[...] = twice_across(r.third)
+    mix = r.mix[...]
+    r.mix_t[...] = mix.astype(F32).T.astype(BF16)
+    r.mix_two[...] = jnp.concatenate([mix, mix], 1)
+    head = jnp.broadcast_to(r.head[...].astype(F32), (128, 128)).T
+    r.head_t[...] = jnp.concatenate([head] * 4, 1)
+    kinds = r.species[...]
+    base = jnp.zeros((1, A), F32)
+    for k in range(SPECIES):
+        base = base + jnp.where(kinds == k, r.shift[k], 0.0)
+    r.base[...] = base
     count = r.count[0, 0, 0]
 
     for b in range(STEPS):
@@ -309,12 +321,10 @@
     bump = jnp.exp(-(away * away) / CUT)
     basis = bump * envelope
     d_basis = bump * (d_envelope - (2.0 / CUT) * away * envelope)
-    first = twice_across(r.first)
-    z = dot(first, jnp.concatenate([stack_high_low(basis), stack_high_low(d_basis)], 1))
+    z = dot(r.first_t[...], jnp.concatenate([stack_high_low(basis), stack_high_low(d_basis)], 1))
     h, slope = silu_parts(z[:, :NP])
     d = slope * z[:, NP:]
-    second = twice_across(r.second)
-    z = dot(second, jnp.concatenate([stack_high_low(h), stack_high_low(d)], 1))
+    z = dot(r.second_t[...], jnp.concatenate([stack_high_low(h), stack_high_low(d)], 1))
     h, slope = silu_parts(z[:, :NP])
     d = slope * z[:, NP:]
     r.hidden[0] = stack_high_low(h)
@@ -325,7 +335,6 @@
 
 
 def scatter(r):
-    third = twice_across(r.third)
     v = r.geom[4:7, :]
     ux, uy, uz = 0.5 * v[0:1], 0.5 * v[1:2], 0.5 * v[2:3]
     harmonics = [None, ux, uy, uz] + harmonics_of(ux, uy, uz)
@@ -336,9 +345,9 @@
                 order = 0 if i == 0 else (1 if i < 4 else 2)
                 part = slice(CH * order, CH * (order + 1))
                 if i in (0, 1, 4):
-                    z = dot(third[part], r.hidden[0, :, lanes])
+                    z = dot(r.third_t[part, :], r.hidden[0, :, lanes])
                     r.radial[b, part, :] = z * r.feats[:, lanes]
-                    z = dot(third[part], r.hidden[1, :, lanes])
+                    z = dot(r.third_t[part, :], r.hidden[1, :, lanes])
                     r.slope[b, part, :] = z * r.feats[:, lanes]
                 term = r.radial[b, part, :]
                 if i:
@@ -362,15 +371,13 @@
             total = total + moment(i) * moment(i)
         squares.append(total)
     invariants = jnp.concatenate([moment(0)] + squares, 0)
-    mix = r.mix[...]
-    mix_t = mix.astype(F32).T.astype(BF16)
     high, low = high_low(invariants)
+    mix_t = r.mix_t[...]
     mixed = dot(mix_t, high.astype(BF16)) + dot(mix_t, low.astype(BF16))
-    head = jnp.broadcast_to(r.head[...].astype(F32), (128, 128)).T
-    head = jnp.concatenate([head] * 4, 1)
+    head = r.head_t[...]
     h, slope = silu_parts(mixed)
     d_mixed = stack_high_low(head * slope)
-    d_inv = dot(jnp.concatenate([mix, mix], 1), d_mixed)
+    d_inv = dot(r.mix_two[...], d_mixed)
     for i in range(9):
         order = 0 if i == 0 else (1 if i < 4 else 2)
         grad = d_inv[CH * order : CH * (order + 1)]
@@ -379,11 +386,7 @@
         high, low = high_low(grad)
         r.grads[CH * i : CH * (i + 1), 0:AP] = high.astype(BF16)
         r.grads[CH * i : CH * (i + 1), AP : 2 * AP] = low.astype(BF16)
-    energy = jnp.sum(head * h, axis=0, keepdims=True)[:, :A]
-    kinds = r.species[...]
-    for k in range(SPECIES):
-        energy = energy + jnp.where(kinds == k, r.shift[k], 0.0)
-    r.out[0] = energy
+    r.out[0] = jnp.sum(head * h, axis=0, keepdims=True)[:, :A] + r.base[...]
 
 
 def pulls(r):
@@ -452,7 +455,16 @@
     "count": ((1, 1, 1), jnp.int32),
     "shift": ((SPECIES,), F32),
 }
+EARLY = ("pos", "list", "feat")
 WORK = {
+    "first_t": ((RH, 2 * NRB), BF16),
+    "second_t": ((RH, 2 * RH), BF16),
+    "third_t": ((3 * CH, 2 * RH), BF16),
+    "mix_t": ((CH, 3 * CH), BF16),
+    "mix_two": ((3 * CH, 2 * CH), BF16),
+    "head_t": ((CH, AP), F32),
+    "base": ((1, A), F32),
+    "upper": ((A, A), BF16),
     "own_table": ((CH + 16, AP), BF16),
     "table": ((CH + 16, GT), BF16),
     "keys": ((GT, BL), jnp.int32),
@@ -475,7 +487,7 @@
     "pick": ((GT, A), BF16),
     "sent": ((SENT, CH), BF16),
     "got": ((SENT, CH), BF16),
-    "returned": ((26, 8, 128), F32),
+    "returned": ((26, 4, 128), F32),
 }
 INPUTS = ["hbm_" + name for name in LOADS]
 NAMES = INPUTS + ["out"] + list(LOADS) + list(WORK)
@@ -485,14 +497,19 @@
 def kernel(*refs):
     r = Refs(NAMES, refs)
     at = neighbours()
-    barrier = enter(at)
     loads = {}
     for i, name in enumerate(LOADS):
         loads[name] = pltpu.make_async_copy(
             getattr(r, "hbm_" + name), getattr(r, name), r.load_sem.at[i]
         )
-        loads[name].start()
-    for name in ("pos", "feat", "list"):
+        if name in EARLY:
+            loads[name].start()
+    barrier = enter(at)
+    for name in LOADS:
+        if name not in EARLY:
+            loads[name].start()
+    r.upper[...] = (iota((A, A), 0) <= iota((A, A), 1)).astype(BF16)
+    for name in EARLY:
         loads.pop(name).wait()
     copies = {}
 
@@ -512,7 +529,7 @@
             )
             copies[i].start()
 
-    choose(r.pos, r.feat, r.list, r.pick, r.sent, send)
+    choose(r.pos, r.feat, r.list, r.upper, r.pick, r.sent, send)
     for copy in loads.values():
         copy.wait()
     prepare(r)
@@ -534,7 +551,7 @@
                 continue
             start = lane // 128 * 128
             returns[i] = pltpu.make_async_remote_copy(
-                src_ref=r.ghost.at[:, start : start + 128],
+                src_ref=r.ghost.at[0:4, start : start + 128],
                 dst_ref=r.returned.at[i],
                 send_sem=r.back_send_sem.at[i],
                 recv_sem=r.back_recv_sem.at[i],
@@ -542,7 +559,7 @@
                 device_id_type=MESH,
             )
             returns[i].start()
-    total = own_forces(r)[:, :A]
+    total = own_forces(r)[:4, :A]
     for copy in copies.values():
         copy.wait_send()
     for half in (NEAR, FAR):
@@ -554,7 +571,7 @@
             tiles.append(group_lanes(got, 128 // len(members)))
         got = stack_high_low(jnp.concatenate(tiles, 1))
         sums = dot(got, r.pick[HALF * half : HALF * (half + 1), :])
-        total = total + sums[:8] + sums[8:]
+        total = total + sums[:4] + sums[4:]
     for axis in range(3):
         r.out[axis + 1] = total[axis : axis + 1]
     for copy in returns.values():

time: 37.3 us -> 37.2 us (level)
  no operation moved by 1% of the time
where the time goes in v5:
time: 37.2 us; the launch traced here: 37.1 us
  Pallas kernels  35.8 us (96%)
  between operations  1.29 us (3%)
    pallas_call x1, Pallas kernels, shards(): pl.pallas_call(kernel, out_shape=pltpu.VMEM((4, 1, A), F32), in_specs=[pl...  35.2 us

profile of v5, /device:TPU:1, one launch (start us, length us, event | category | flops | bytes accessed | tf_op | source)
XLA Modules:
  0.0 37.1 jit_solution(16712640208665979522)
XLA Ops:
  1.3 35.2 %layer.1.both_ref = f32[4,1,432]{2,1,0:T(1,128)S(1)} custom-call(bf16[3,432]{1,0:T(4,128)(2,1)} %bitcast.16, bf16[432,128]{1,0:T(8,128)(2,1)} %bitcast.13, s32[1,304]{1,0:T(1,128)} %bitcast.18, s32[10,1,128]{2,1,0:T(1,128)} %bitcast.14, s32[10,1,128]{2,1,0:T(1,128)} %bitcast.15, bf16[8,64]{1,0:T(8,128)(2,1)} %refs_5_.1, bf16[64,64]{1,0:T(8,128)(2,1)} %refs_6_.1, ...), custom_call_target="tpu_custom_call" | custom-call | tf_op jit(solution)/shard_map/layer/pallas_call | solution.py:613
  36.5 0.6 %split.1 = (f32[1,1,432]{2,1,0:T(1,128)}, f32[3,1,432]{2,1,0:T(1,128)}) custom-call(f32[4,1,432]{2,1,0:T(1,128)S(1)} %layer.1.both_ref), custom_call_target="tpu_custom_call" | custom-call | tf_op jit(solution)/shard_map/split/pallas_call | solution.py:644

commit v6 on v5

--- a/solution.py
+++ b/solution.py
@@ -347,8 +347,6 @@
                 if i in (0, 1, 4):
                     z = dot(r.third_t[part, :], r.hidden[0, :, lanes])
                     r.radial[b, part, :] = z * r.feats[:, lanes]
-                    z = dot(r.third_t[part, :], r.hidden[1, :, lanes])
-                    r.slope[b, part, :] = z * r.feats[:, lanes]
                 term = r.radial[b, part, :]
                 if i:
                     term = term * harmonics[i][:, lanes]
@@ -391,6 +389,7 @@
 
 def pulls(r):
     for b in range(STEPS):
+        d = dot(r.third_t[...], r.hidden[1, :, span(b)])
         r.back[b] = dot(r.grads[...], r.to_own[b])
         v = r.geom[4:7, span(b)]
         along, across = [], []
@@ -400,7 +399,7 @@
             grad = r.back[b, CH * i : CH * (i + 1), :]
             if order:
                 along.append(jnp.sum(r.radial[b, part, :] * grad, axis=0, keepdims=True))
-            slope = r.slope[b, part, :]
+            slope = d[part] * r.feats[:, span(b)]
             across.append(jnp.sum(slope * grad, axis=0, keepdims=True))
         x, y, z = 0.5 * v[0:1], 0.5 * v[1:2], 0.5 * v[2:3]
         ax, ay, az, b0, b1, b2, b3, b4 = along
@@ -477,7 +476,6 @@
     "geom": ((8, NP), F32),
     "hidden": ((2, 2 * RH, NP), BF16),
     "radial": ((STEPS, 3 * CH, BL), F32),
-    "slope": ((STEPS, 3 * CH, BL), F32),
     "terms": ((9 * CH, STEPS * 2 * BL), BF16),
     "moments": ((9 * CH, AP), F32),
     "grads": ((9 * CH, 2 * AP), BF16),

time: 37.2 us -> 37.1 us (level)
  no operation moved by 1% of the time
where the time goes in v6:
time: 37.1 us; the launch traced here: 37 us
  Pallas kernels  35.7 us (96%)
  between operations  1.29 us (3%)
    pallas_call x1, Pallas kernels, shards(): pl.pallas_call(kernel, out_shape=pltpu.VMEM((4, 1, A), F32), in_specs=[pl...  35.1 us

profile of v6, /device:TPU:1, one launch (start us, length us, event | category | flops | bytes accessed | tf_op | source)
XLA Modules:
  0.0 37.0 jit_solution(11739139091230067739)
XLA Ops:
  1.3 35.1 %layer.1.both_ref = f32[4,1,432]{2,1,0:T(1,128)S(1)} custom-call(bf16[3,432]{1,0:T(4,128)(2,1)} %bitcast.16, bf16[432,128]{1,0:T(8,128)(2,1)} %bitcast.13, s32[1,304]{1,0:T(1,128)} %bitcast.18, s32[10,1,128]{2,1,0:T(1,128)} %bitcast.14, s32[10,1,128]{2,1,0:T(1,128)} %bitcast.15, bf16[8,64]{1,0:T(8,128)(2,1)} %refs_5_.1, bf16[64,64]{1,0:T(8,128)(2,1)} %refs_6_.1, ...), custom_call_target="tpu_custom_call" | custom-call | tf_op jit(solution)/shard_map/layer/pallas_call | solution.py:611
  36.4 0.6 %split.1 = (f32[1,1,432]{2,1,0:T(1,128)}, f32[3,1,432]{2,1,0:T(1,128)}) custom-call(f32[4,1,432]{2,1,0:T(1,128)S(1)} %layer.1.both_ref), custom_call_target="tpu_custom_call" | custom-call | tf_op jit(solution)/shard_map/split/pallas_call | solution.py:642

commit v7 on v6

--- a/solution.py
+++ b/solution.py
@@ -495,6 +495,7 @@
 def kernel(*refs):
     r = Refs(NAMES, refs)
     at = neighbours()
+    barrier = enter(at)
     loads = {}
     for i, name in enumerate(LOADS):
         loads[name] = pltpu.make_async_copy(
@@ -502,7 +503,6 @@
         )
         if name in EARLY:
             loads[name].start()
-    barrier = enter(at)
     for name in LOADS:
         if name not in EARLY:
             loads[name].start()

time: 37.1 us -> 37.1 us (level)
  no operation moved by 1% of the time
where the time goes in v7:
time: 37.1 us; the launch traced here: 37 us
  Pallas kernels  35.7 us (96%)
  between operations  1.29 us (3%)
    pallas_call x1, Pallas kernels, shards(): pl.pallas_call(kernel, out_shape=pltpu.VMEM((4, 1, A), F32), in_specs=[pl...  35.1 us

profile of v7, /device:TPU:1, one launch (start us, length us, event | category | flops | bytes accessed | tf_op | source)
XLA Modules:
  0.0 37.0 jit_solution(2485191613232255745)
XLA Ops:
  1.3 35.1 %layer.1.both_ref = f32[4,1,432]{2,1,0:T(1,128)S(1)} custom-call(bf16[3,432]{1,0:T(4,128)(2,1)} %bitcast.16, bf16[432,128]{1,0:T(8,128)(2,1)} %bitcast.13, s32[1,304]{1,0:T(1,128)} %bitcast.18, s32[10,1,128]{2,1,0:T(1,128)} %bitcast.14, s32[10,1,128]{2,1,0:T(1,128)} %bitcast.15, bf16[8,64]{1,0:T(8,128)(2,1)} %refs_5_.1, bf16[64,64]{1,0:T(8,128)(2,1)} %refs_6_.1, ...), custom_call_target="tpu_custom_call" | custom-call | tf_op jit(solution)/shard_map/layer/pallas_call | solution.py:611
  36.4 0.6 %split.1 = (f32[1,1,432]{2,1,0:T(1,128)}, f32[3,1,432]{2,1,0:T(1,128)}) custom-call(f32[4,1,432]{2,1,0:T(1,128)S(1)} %layer.1.both_ref), custom_call_target="tpu_custom_call" | custom-call | tf_op jit(solution)/shard_map/split/pallas_call | solution.py:642
